TPU v7x, 32 devices: a whole 2x2x4 slice. The times are simulated.
32 devices in a mesh: dp: 8 (over z, y), tensor: 4 (over x, core).
Axes of the slice: x: 2, y: 2, z: 4, core: 2. Of those that a mesh axis runs over, the one named last changes fastest.
Arguments:
- tokens: bfloat16 [16384, 1280], P(('dp', 'tensor')), may hold values from -6 to 6
- cotangent: bfloat16 [16384, 1280], P(('dp', 'tensor')), may hold values from -6 to 6
- lengths: int32 [16], P('dp'), may hold values from 256 to 1024, as said below
- key_mask: int32 [16, 1024], P('dp'), may hold values 0 or 1
- qkv_weight: float32 [1280, 3, 1280], P('dp', None, 'tensor'), may hold values from -0.15625 to 0.15625
- out_weight: float32 [1280, 1280], P(('tensor', 'dp')), may hold values from -4 to 4
- up_weight: float32 [1280, 5120], P('dp', 'tensor'), may hold values from -0.15625 to 0.15625
- down_weight: float32 [5120, 1280], P(('tensor', 'dp')), may hold values from -0.078125 to 0.078125
- norm_params: float32 [4, 1280], P(None, 'dp')
- qkv_first: float32 [1280, 3, 1280], P('dp', None, 'tensor'), may hold values from -0.001953125 to 0.001953125
- qkv_second: float32 [1280, 3, 1280], P('dp', None, 'tensor'), may hold values from 5.493164e-08 to 9.155273e-07
- out_first: float32 [1280, 1280], P(('tensor', 'dp')), may hold values from -0.00010681152 to 0.00010681152
- out_second: float32 [1280, 1280], P(('tensor', 'dp')), may hold values from 1.4038086e-10 to 2.2583009e-09
- up_first: float32 [1280, 5120], P('dp', 'tensor'), may hold values from -0.00024414062 to 0.00024414062
- up_second: float32 [1280, 5120], P('dp', 'tensor'), may hold values from 1.1596679e-09 to 4.577637e-09
- down_first: float32 [5120, 1280], P(('tensor', 'dp')), may hold values from -0.0004272461 to 0.0004272461
- down_second: float32 [5120, 1280], P(('tensor', 'dp')), may hold values from 3.2958984e-09 to 1.3183594e-08
- norm_first: float32 [4, 1280], P(None, 'dp'), may hold values from -0.0029296875 to 0.0029296875
- norm_second: float32 [4, 1280], P(None, 'dp'), may hold values from 1.2207032e-07 to 2.0141601e-06
Outputs:
- layer_out: bfloat16 [16384, 1280], P(('dp', 'tensor'))
- input_grad: bfloat16 [16384, 1280], P(('dp', 'tensor'))
- grad_norm: float32 [], replicated
- qkv_new: float32 [1280, 3, 1280], P('dp', None, 'tensor')
- qkv_first_new: float32 [1280, 3, 1280], P('dp', None, 'tensor')
- qkv_second_new: float32 [1280, 3, 1280], P('dp', None, 'tensor')
- out_new: float32 [1280, 1280], P(('tensor', 'dp'))
- out_first_new: float32 [1280, 1280], P(('tensor', 'dp'))
- out_second_new: float32 [1280, 1280], P(('tensor', 'dp'))
- up_new: float32 [1280, 5120], P('dp', 'tensor')
- up_first_new: float32 [1280, 5120], P('dp', 'tensor')
- up_second_new: float32 [1280, 5120], P('dp', 'tensor')
- down_new: float32 [5120, 1280], P(('tensor', 'dp'))
- down_first_new: float32 [5120, 1280], P(('tensor', 'dp'))
- down_second_new: float32 [5120, 1280], P(('tensor', 'dp'))
- norm_new: float32 [4, 1280], P(None, 'dp')
- norm_first_new: float32 [4, 1280], P(None, 'dp')
- norm_second_new: float32 [4, 1280], P(None, 'dp')
- shift_grad: float32 [1280], P('dp')
Inputs may be any that keep to these rules, and one draw needn't show every extreme that they name: `lengths`: tokens that count in each cell, from its first position; some cell has all 1024 in every draw.
All inputs are finite; a program needn't handle non-finite values. No bound on the sum of `key_mask` on one device may be relied on, other than what follows from the above.
Results may differ from a plain program's by a relative error of at most 0.02.
Values may be sent and summed in bfloat16 or wider, within the bound.
No kernel may reach another device: no remote copies, remote signals or barrier semaphores. Data moves between devices by JAX's collectives and lax.ppermute only.
A program may use at most 192 MiB of HBM per device.

v0:
```python
import functools

import jax
import jax.numpy as jnp
from jax import lax
from jax.experimental import pallas as pl
from jax.experimental.layout import Layout, with_layout_constraint
from jax.experimental.pallas import tpu as pltpu
from jax.sharding import PartitionSpec as P

HD = 64
STEP = 5

NORM_EPS = 1e-05
CLIP_LIMIT = 1.0
BETA_FIRST = 0.5
BETA_SECOND = 0.5
ADAM_EPS = 1e-08
DECAY_RATE = 0.01
RATE_QKV = 0.03
RATE_OUT = 0.5
RATE_UP = 0.03
RATE_DOWN = 0.015
RATE_NORM = 0.2

F32 = jnp.float32
BF16 = jnp.bfloat16
NN = (((1,), (0,)), ((), ()))
NT = (((1,), (1,)), ((), ()))
TN = (((0,), (0,)), ((), ()))
VMEM = pl.BlockSpec(memory_space=pltpu.VMEM)


def dot(left, right, dims=NN):
    return lax.dot_general(left, right, dims, preferred_element_type=F32)


def widen(block, columns, lane):
    rows = block.shape[0]
    wide = jnp.concatenate([block.astype(F32), jnp.zeros((rows, HD), F32)], axis=1)
    for n, column in enumerate(columns):
        wide = jnp.where(lane == HD + n, column, wide)
    return wide.astype(BF16)


def minus_parts(column):
    high = column.astype(BF16).astype(F32)
    rest = column - high
    middle = rest.astype(BF16).astype(F32)
    return [-high, -middle, middle - rest]


def attend_kernel(heads, step, one_ref, weight_ref, bias_ref, qkv_ref, ctx_ref, lse_ref, keys):
    tokens = qkv_ref.shape[0]
    width = heads * HD
    lane = lax.broadcasted_iota(jnp.int32, (1, 2 * HD), 1)

    def project(n, _):
        rows = pl.ds(pl.multiple_of(n * step, step), step)
        qkv_ref[rows, :] = dot(one_ref[rows, :], weight_ref[...]).astype(BF16)
        return 0

    lax.fori_loop(0, tokens // step, project, 0)
    bias = bias_ref[...].T[:, 0:1]
    for h in range(heads):
        keys[h] = widen(qkv_ref[:, width + h * HD : width + (h + 1) * HD], [bias], lane)

    def block(n, _):
        rows = pl.ds(pl.multiple_of(n * step, step), step)
        outs = []
        stat = jnp.zeros((step, 2 * HD), F32)
        for h in range(heads):
            query = qkv_ref[rows, h * HD : (h + 1) * HD].astype(F32) * HD ** (-0.5)
            scores = dot(widen(query, [jnp.ones((step, 1), F32)], lane), keys[h], NT)
            top = jnp.max(scores, axis=1, keepdims=True)
            weights = jnp.exp(scores - top)
            total = jnp.sum(weights, axis=1, keepdims=True)
            values = qkv_ref[:, 2 * width + h * HD : 2 * width + (h + 1) * HD]
            outs.append((dot(weights.astype(BF16), values) / total).astype(BF16))
            stat = jnp.where(lane == h, top + jnp.log(total), stat)
        ctx_ref[rows, :] = jnp.concatenate(outs, axis=1)
        lse_ref[rows, :] = stat
        return 0

    lax.fori_loop(0, tokens // step, block, 0)


def attend(one, weight, bias, heads, step=1024):
    tokens = one.shape[0]
    return pl.pallas_call(
        functools.partial(attend_kernel, heads, step),
        out_shape=(
            jax.ShapeDtypeStruct((tokens, 3 * heads * HD), BF16),
            jax.ShapeDtypeStruct((tokens, heads * HD), BF16),
            jax.ShapeDtypeStruct((tokens, 2 * HD), F32),
        ),
        in_specs=[VMEM] * 3,
        out_specs=[VMEM] * 3,
        scratch_shapes=[pltpu.VMEM((heads, tokens, 2 * HD), BF16)],
        compiler_params=pltpu.CompilerParams(vmem_limit_bytes=48 * 2**20),
        cost_estimate=pl.CostEstimate(flops=0, bytes_accessed=1, transcendentals=0),
        name="attend",
    )(one, weight, bias)


def attend_back_kernel(
    heads,
    step,
    qkv_ref,
    bias_ref,
    ctx_ref,
    lse_ref,
    own_ref,
    mate_ref,
    weight_ref,
    out_ref,
    keys,
    values,
    dk,
    dv,
    grad_ref,
):
    tokens = qkv_ref.shape[0]
    width = heads * HD
    scale = HD ** (-0.5)
    lane = lax.broadcasted_iota(jnp.int32, (1, 2 * HD), 1)
    one = jnp.ones((tokens, 1), F32)
    bias = bias_ref[...].T[:, 0:1]
    half = tokens // 2
    for n, ref in enumerate((own_ref, mate_ref)):
        grad_ref[n * half : (n + 1) * half, :] = dot(ref[...], weight_ref[...], NT).astype(BF16)
    for h in range(heads):
        key = qkv_ref[:, width + h * HD : width + (h + 1) * HD]
        value = qkv_ref[:, 2 * width + h * HD : 2 * width + (h + 1) * HD]
        keys[h] = widen(key, [bias, one, one, one], lane)
        values[h] = widen(value, [one, one, one], lane)
    dk[...] = jnp.zeros_like(dk)
    dv[...] = jnp.zeros_like(dv)

    def block(n, _):
        rows = pl.ds(pl.multiple_of(n * step, step), step)
        outs = []
        ones = jnp.ones((step, 1), F32)
        for h in range(heads):
            cols = slice(h * HD, (h + 1) * HD)
            query = qkv_ref[rows, cols].astype(F32) * scale
            grad = grad_ref[rows, cols].astype(F32)
            delta = jnp.sum(grad * ctx_ref[rows, cols].astype(F32), axis=1, keepdims=True)
            lse = lse_ref[rows, h : h + 1]
            weights = jnp.exp(dot(widen(query, [ones] + minus_parts(lse), lane), keys[h], NT))
            slopes = dot(widen(grad, minus_parts(delta), lane), values[h], NT)
            slopes = (weights * slopes).astype(BF16)
            weights = weights.astype(BF16)
            key = qkv_ref[:, width + h * HD : width + (h + 1) * HD]
            outs.append((dot(slopes, key) * scale).astype(BF16))
            dk[h] += dot(query.T.astype(BF16), slopes)
            dv[h] += dot(grad.T.astype(BF16), weights)
        out_ref[rows, :width] = jnp.concatenate(outs, axis=1)
        return 0

    lax.fori_loop(0, tokens // step, block, 0)
    for place, total in ((1, dk), (2, dv)):
        turned = jnp.concatenate([total[h].T for h in range(heads)], axis=1)
        out_ref[:, place * width : (place + 1) * width] = turned.astype(BF16)


def attend_back(qkv, bias, ctx, lse, own, mate, weight, heads, step=1024):
    tokens = qkv.shape[0]
    return pl.pallas_call(
        functools.partial(attend_back_kernel, heads, step),
        out_shape=jax.ShapeDtypeStruct((tokens, 3 * heads * HD), BF16),
        in_specs=[VMEM] * 7,
        out_specs=VMEM,
        scratch_shapes=[pltpu.VMEM((heads, tokens, 2 * HD), BF16)] * 2
        + [pltpu.VMEM((heads, HD, tokens), F32)] * 2
        + [pltpu.VMEM((tokens, heads * HD), BF16)],
        compiler_params=pltpu.CompilerParams(vmem_limit_bytes=48 * 2**20),
        cost_estimate=pl.CostEstimate(flops=0, bytes_accessed=1, transcendentals=0),
        name="attend_back",
    )(qkv, bias, ctx, lse, own, mate, weight)


def swap(value, axis, bits):
    size = lax.axis_size(axis)
    return lax.ppermute(value, axis, [(i, i ^ bits) for i in range(size)])


def core_swap(value):
    return swap(value, "tensor", 1)


def side_swap(value):
    return swap(value, "tensor", 2)


def tie(*values):
    return lax.optimization_barrier(values)


def dp_split(size):
    fast = 2 if size < 16 else 4
    return size // fast, fast


def high_swap(value, k):
    return swap(value, "dp", k * dp_split(lax.axis_size("dp"))[1])


def gather_small(shard):
    size = lax.axis_size("dp")
    blocks = shard[None]
    bits = 1
    while bits < size:
        blocks = jnp.concatenate([blocks, swap(blocks, "dp", bits)])
        bits *= 2
    index = lax.axis_index("dp")
    return jnp.stack([blocks[index ^ n] for n in range(size)])


def spread(block):
    _, fast = dp_split(lax.axis_size("dp"))
    return [block] + [swap(block, "dp", j) for j in range(1, fast)]


def entries(k, line, at=None):
    return [(k, j, block, at if j else None) for j, block in enumerate(line)]


def joined_entries(ks, blocks, others):
    return [
        entry
        for n, (k, block) in enumerate(zip(ks, blocks, strict=True))
        for entry in entries(k, [block, *others], n)
    ]


def pack_kernel(qkv_ref, out_ref, packed_ref):
    rows, width = out_ref.shape
    step = width * rows // qkv_ref.shape[1]
    parts = [qkv_ref[n] for n in range(qkv_ref.shape[0])]
    turned = [out_ref[:, n : n + step] for n in range(0, width, step)]
    packed = jnp.concatenate([*parts, jnp.concatenate(turned, axis=0)], axis=1)
    packed_ref[...] = packed.astype(BF16)


def pack_first(qkv, out):
    rows = qkv.shape[1]
    shape = (rows, qkv.shape[0] * qkv.shape[2] + out.size // rows)
    if out.shape[0] % 8:
        step = out.shape[1] * out.shape[0] // rows
        turned = jnp.concatenate([out[:, n : n + step] for n in range(0, out.shape[1], step)])
        return jnp.concatenate([*qkv, turned], axis=1).astype(BF16)
    return pl.pallas_call(
        pack_kernel,
        out_shape=jax.ShapeDtypeStruct(shape, BF16),
        in_specs=[VMEM] * 2,
        out_specs=VMEM,
        compiler_params=pltpu.CompilerParams(vmem_limit_bytes=16 * 2**20),
        cost_estimate=pl.CostEstimate(flops=0, bytes_accessed=1, transcendentals=0),
        name="pack_first",
    )(qkv, out)


def assemble(blocks, cut=None):
    slow, fast = dp_split(lax.axis_size("dp"))
    rows, columns = blocks[0][2].shape[-2:]
    kind = blocks[0][2].dtype
    index = lax.axis_index("dp")
    place = jnp.stack([index // fast, index % fast]).astype(jnp.int32)
    where = [(k, j, at) for k, j, _, at in blocks]
    out_rows = rows * (columns - cut) // columns if cut else 0

    def kernel(place_ref, *refs):
        ins, outs = refs[: len(where)], refs[len(where) : -2]
        whole, sems = refs[-2:] if cut else (outs[0], refs[-1])
        copies = []
        for n, (source, (k, j, at)) in enumerate(zip(ins, where, strict=True)):
            target = (place_ref[0] ^ k) * fast + (place_ref[1] ^ j)
            source = source if at is None else source.at[at]
            copies.append(pltpu.make_async_copy(source, whole.at[target], sems.at[n]))
        for copy in copies:
            copy.start()
        for copy in copies:
            copy.wait()
        if cut:
            outs[0][...] = whole[:, :, :cut]
            if out_rows % 8:
                outs[1][...] = whole[:, :, cut:]
            else:
                turned = []
                for n in range(slow * fast):
                    block = whole[n, :, cut:].astype(F32)
                    parts = [block[m : m + out_rows] for m in range(0, rows, out_rows)]
                    turned.append(jnp.concatenate(parts, axis=1))
                outs[1][...] = jnp.concatenate(turned, axis=0).astype(kind)

    size = slow * fast
    full = (size, rows, columns)
    if not cut:
        shapes = [full]
    elif out_rows % 8:
        shapes = [(size, rows, cut), (size, rows, columns - cut)]
    else:
        shapes = [(size, rows, cut), (size * out_rows, columns)]
    outs = pl.pallas_call(
        kernel,
        out_shape=[jax.ShapeDtypeStruct(shape, kind) for shape in shapes],
        in_specs=[pl.BlockSpec(memory_space=pltpu.SMEM)]
        + [pl.BlockSpec(memory_space=pltpu.HBM)] * len(where),
        out_specs=[VMEM] * len(shapes),
        scratch_shapes=[
            pltpu.VMEM(full if cut else (8, 16, 128), kind),
            pltpu.SemaphoreType.DMA((len(where),)),
        ],
        compiler_params=pltpu.CompilerParams(vmem_limit_bytes=24 * 2**20),
        cost_estimate=pl.CostEstimate(flops=0, bytes_accessed=1, transcendentals=0),
        name="assemble",
    )(place, *[array for _, _, array, _ in blocks])
    outs = list(outs)
    if cut and out_rows % 8:
        turned = outs[1].reshape(size, rows // out_rows, out_rows, columns - cut)
        outs[1] = turned.transpose(0, 2, 1, 3).reshape(size * out_rows, columns)
    return [out.reshape(-1, out.shape[-1]) for out in outs]


def pick(total, k, j):
    slow, fast = dp_split(lax.axis_size("dp"))
    rows = total.shape[0] // (slow * fast)
    index = lax.axis_index("dp")
    start = (((index // fast) ^ k) * fast + ((index % fast) ^ j)) * rows
    return lax.dynamic_slice_in_dim(total, start, rows, 0)


def rows_first(value):
    return with_layout_constraint(value, Layout(tuple(range(value.ndim))))


def scatter_send(total, ks):
    _, fast = dp_split(lax.axis_size("dp"))
    return [
        swap(jnp.concatenate([rows_first(pick(total, k, j)) for k in ks]), "dp", j)
        for j in range(1, fast)
    ]


def scatter_lines(total, ks, received):
    lines = {}
    for n, k in enumerate(ks):
        line = pick(total, k, 0).astype(F32)
        rows = line.shape[0]
        for part in received:
            line = line + part[n * rows : (n + 1) * rows].astype(F32)
        lines[k] = rows_first(line.astype(BF16))
    return lines


def relay_ks():
    slow, _ = dp_split(lax.axis_size("dp"))
    return [1, *range(2, slow, 2)], [*range(3, slow, 2), 0]


def relay_send(lines):
    ks, _ = relay_ks()
    return high_swap(jnp.concatenate([lines[k] for k in ks]), 1)


def relay_split(received):
    ks, _ = relay_ks()
    rows = received.shape[0] // len(ks)
    return {k: received[n * rows : (n + 1) * rows] for n, k in enumerate(ks)}


def relay_last(lines, received):
    _, ks = relay_ks()
    got = relay_split(received)
    parts = [lines[0], got[1]]
    for k in ks[:-1]:
        line = lines[k].astype(F32) + got[k ^ 1].astype(F32)
        parts.append(high_swap(line.astype(BF16), k))
    return parts


def parts_sum(parts):
    return functools.reduce(jnp.add, [part.astype(F32) for part in parts])


def cores_sum(left, right, dims=NN):
    return own_sum(left, right, mates_part(left, right, dims), dims)


def mates_part(left, right, dims=NN):
    return core_swap(dot(left[left.shape[0] // 2 :], right, dims).astype(BF16))


def own_sum(left, right, mate, dims=NN):
    return dot(left[: left.shape[0] // 2], right, dims) + mate.astype(F32)


def side_send(value):
    half = value.shape[0] // 2
    return [side_swap(value[:half]), side_swap(value[half:])]


def join(parts):
    return jnp.concatenate(parts)


def with_mate(own):
    return jnp.concatenate([own, core_swap(own)])


def norm_kernel(step, *refs):
    *pieces, rows_ref, out_ref = refs
    gain, shift = rows_ref[0:1, :], rows_ref[1:2, :]
    at = 0
    for ref in pieces:
        for start in range(0, ref.shape[0], step):
            values = ref[start : start + step, :].astype(F32)
            centered = values - jnp.mean(values, axis=-1, keepdims=True)
            inverse = lax.rsqrt(jnp.mean(centered * centered, axis=-1, keepdims=True) + NORM_EPS)
            out_ref[at : at + step, :] = (centered * inverse * gain + shift).astype(BF16)
            at += step


def norm_tokens(pieces, rows, step=128):
    size, width = sum(v.shape[0] for v in pieces), pieces[0].shape[1]
    return pl.pallas_call(
        functools.partial(norm_kernel, step),
        out_shape=jax.ShapeDtypeStruct((size, width), BF16),
        in_specs=[VMEM] * (len(pieces) + 1),
        out_specs=VMEM,
        compiler_params=pltpu.CompilerParams(vmem_limit_bytes=24 * 2**20),
        cost_estimate=pl.CostEstimate(flops=0, bytes_accessed=1, transcendentals=0),
        name="norm_tokens",
    )(*pieces, rows)


def weight_grad_kernel(count, *refs):
    lefts, rights, out_ref = refs[:count], refs[count:-1], refs[-1]
    total = None
    at = 0
    for left in lefts:
        for start in range(0, left.shape[0], rights[0].shape[0]):
            right = rights[at]
            at += 1
            term = dot(left[start : start + right.shape[0], :], right[...], TN)
            total = term if total is None else total + term
    out_ref[...] = total.astype(BF16)


def weight_grad(lefts, rights, step=256):
    rows, columns = lefts[0].shape[1], rights[0].shape[1]
    return pl.pallas_call(
        functools.partial(weight_grad_kernel, len(lefts)),
        grid=(rows // step,),
        out_shape=jax.ShapeDtypeStruct((rows, columns), BF16),
        in_specs=[pl.BlockSpec((v.shape[0], step), lambda i: (0, i)) for v in lefts]
        + [pl.BlockSpec(v.shape, lambda i: (0, 0)) for v in rights],
        out_specs=pl.BlockSpec((step, columns), lambda i: (i, 0)),
        compiler_params=pltpu.CompilerParams(vmem_limit_bytes=40 * 2**20),
        cost_estimate=pl.CostEstimate(flops=0, bytes_accessed=1, transcendentals=0),
        name="weight_grad",
    )(*lefts, *rights)


def sum_all(value):
    size = lax.axis_size("dp")
    value = value + core_swap(value)
    steps = [("tensor", 2)] + [("dp", 1 << n) for n in range(size.bit_length() - 1)]
    for n in range(0, len(steps), 2):
        first = steps[n]
        if n + 1 == len(steps):
            value = value + swap(value, *first)
            continue
        second = steps[n + 1]
        if first[0] == second[0]:
            both = swap(value, first[0], first[1] | second[1])
        else:
            tensor = lax.axis_size("tensor")
            bits = first[1] | second[1] * tensor
            pairs = [(i, i ^ bits) for i in range(size * tensor)]
            both = lax.ppermute(value, ("dp", "tensor"), pairs)
        value = (value + swap(value, *first)) + (swap(value, *second) + both)
    return value


def layer_norm_parts(values, gain_row, shift_row):
    centered = values - jnp.mean(values, axis=-1, keepdims=True)
    inverse = lax.rsqrt(jnp.mean(centered * centered, axis=-1, keepdims=True) + NORM_EPS)
    normed = centered * inverse
    return (normed * gain_row + shift_row, normed, inverse)


def layer_norm_back(grad_normed, normed, inverse, gain_row):
    scaled = grad_normed * gain_row
    return inverse * (
        scaled
        - jnp.mean(scaled, axis=-1, keepdims=True)
        - normed * jnp.mean(scaled * normed, axis=-1, keepdims=True)
    )


def adam_update(master, grad_sum, moment_one, moment_two, step_rate, clip_factor):
    clipped = grad_sum * clip_factor
    one_new = BETA_FIRST * moment_one + (1.0 - BETA_FIRST) * clipped
    two_new = BETA_SECOND * moment_two + (1.0 - BETA_SECOND) * clipped * clipped
    one_hat = one_new / (1.0 - BETA_FIRST**STEP)
    two_hat = two_new / (1.0 - BETA_SECOND**STEP)
    master_new = master - step_rate * (
        one_hat / (jnp.sqrt(two_hat) + ADAM_EPS) + DECAY_RATE * master
    )
    return (master_new, one_new, two_new)


def first_back_kernel(tokens_ref, near_ref, far_ref, res_ref, rows_ref, out_ref, sums_ref):
    @pl.when(pl.program_id(0) == 0)
    def _():
        sums_ref[...] = jnp.zeros_like(sums_ref)

    values = tokens_ref[...].astype(F32)
    centered = values - jnp.mean(values, axis=-1, keepdims=True)
    inverse = lax.rsqrt(jnp.mean(centered * centered, axis=-1, keepdims=True) + NORM_EPS)
    normed = centered * inverse
    grad = near_ref[...] + far_ref[...].astype(F32)
    back = layer_norm_back(grad, normed, inverse, rows_ref[0:1, :])
    out_ref[...] = (res_ref[...] + back).astype(BF16)
    width = grad.shape[-1]
    sums_ref[0:8, :] += jnp.sum((grad * normed).reshape(-1, 8, width), axis=0)
    sums_ref[8:16, :] += jnp.sum(grad.reshape(-1, 8, width), axis=0)


def first_back(tokens, near, far, res, rows, step=128):
    size, width = tokens.shape
    block = pl.BlockSpec((step, width), lambda i: (i, 0))
    return pl.pallas_call(
        first_back_kernel,
        grid=(size // step,),
        out_shape=(
            jax.ShapeDtypeStruct((size, width), BF16),
            jax.ShapeDtypeStruct((16, width), F32),
        ),
        in_specs=[block] * 4 + [pl.BlockSpec(rows.shape, lambda i: (0, 0))],
        out_specs=[block, pl.BlockSpec((16, width), lambda i: (0, 0))],
        compiler_params=pltpu.CompilerParams(vmem_limit_bytes=60 * 2**20),
        cost_estimate=pl.CostEstimate(flops=0, bytes_accessed=1, transcendentals=0),
        name="first_back",
    )(tokens, near, far, res, rows)


def squares_kernel(counts, sums_ref, two_ref, early_ref, *refs):
    *parts, out_ref = refs
    width = two_ref.shape[1]
    total = early_ref[...]
    for count in counts:
        value = functools.reduce(jnp.add, [part[...].astype(F32) for part in parts[:count]])
        parts = parts[count:]
        total += jnp.sum(jnp.sum(value * value, axis=0, keepdims=True), axis=1, keepdims=True)
    for n in range(2):
        out_ref[n : n + 1, :width] = jnp.sum(
            sums_ref[8 * n : 8 * n + 8, :], axis=0, keepdims=True
        )
    out_ref[2:4, :width] = two_ref[...]
    out_ref[:, width:] = jnp.broadcast_to(total, (4, 128))


def squares_packed(sums, two, early, gradients):
    return pl.pallas_call(
        functools.partial(squares_kernel, [len(parts) for parts in gradients]),
        out_shape=jax.ShapeDtypeStruct((4, two.shape[1] + 128), F32),
        in_specs=[VMEM] * (3 + sum(len(parts) for parts in gradients)),
        out_specs=VMEM,
        compiler_params=pltpu.CompilerParams(vmem_limit_bytes=24 * 2**20),
        cost_estimate=pl.CostEstimate(flops=0, bytes_accessed=1, transcendentals=0),
        name="squares_packed",
    )(sums, two, early.reshape(1, 1), *[part for parts in gradients for part in parts])


def adam_kernel(rates, counts, packed_ref, *refs):
    *refs, norm_ref, shift_ref = refs
    width = packed_ref.shape[1] - 128
    rows = packed_ref[:, :width]
    squares = jnp.sum(jnp.sum(rows * rows, axis=0, keepdims=True), axis=1, keepdims=True)
    grad_norm = jnp.sqrt(packed_ref[0:1, width : width + 1] + squares)
    clip_factor = jnp.minimum(1.0, CLIP_LIMIT / grad_norm)
    norm_ref[...] = grad_norm
    ins, outs = refs[: -3 * len(rates)], refs[-3 * len(rates) :]
    at = 0
    for n, (rate, count) in enumerate(zip(rates, counts, strict=True)):
        master, one, two = ins[at : at + 3]
        parts = ins[at + 3 : at + 3 + count]
        at += 3 + count
        total = functools.reduce(jnp.add, [part[...].astype(F32) for part in parts])
        results = outs[3 * n : 3 * n + 3]
        if n == len(rates) - 1:
            shift_ref[...] = clip_factor * total[3:4, :]
        if master.ndim == 2:
            for out, value in zip(
                results,
                adam_update(master[...], total, one[...], two[...], rate, clip_factor),
                strict=True,
            ):
                out[...] = value
            continue
        width = master.shape[2]
        for c in range(master.shape[0]):
            grad = total[:, c * width : (c + 1) * width]
            values = adam_update(master[c], grad, one[c], two[c], rate, clip_factor)
            for out, value in zip(results, values, strict=True):
                out[c] = value


def adam_all(packed, weights):
    arrays = [v for master, one, two, parts, _ in weights for v in (master, one, two, *parts)]
    shapes = [master.shape for master, *_ in weights for _ in range(3)]
    shapes += [(1, 1), (1, weights[-1][0].shape[1])]
    outs = pl.pallas_call(
        functools.partial(
            adam_kernel, [rate for *_, rate in weights], [len(w[3]) for w in weights]
        ),
        out_shape=[jax.ShapeDtypeStruct(shape, F32) for shape in shapes],
        in_specs=[VMEM] * (len(arrays) + 1),
        out_specs=[VMEM] * len(shapes),
        compiler_params=pltpu.CompilerParams(vmem_limit_bytes=60 * 2**20),
        name="adam_all",
    )(packed, *arrays)
    return outs[-2], outs[-1], [outs[n : n + 3] for n in range(0, len(outs) - 2, 3)]


def gelu_parts(value):
    share = 0.5 + 0.5 * lax.erf(value * 0.5**0.5)
    slope = share + value * jnp.exp(-0.5 * value * value) * (0.5 / jnp.pi) ** 0.5
    return (value * share).astype(BF16), slope.astype(BF16)


def on_device(
    tokens,
    cotangent,
    lengths,
    key_mask,
    qkv_weight,
    out_weight,
    up_weight,
    down_weight,
    norm_params,
    qkv_first,
    qkv_second,
    out_first,
    out_second,
    up_first,
    up_second,
    down_first,
    down_second,
    norm_first,
    norm_second,
):
    own, width = tokens.shape
    cell = 2 * own
    heads = qkv_weight.shape[2] // HD
    dp, tensor = lax.axis_index("dp"), lax.axis_index("tensor")
    side, core = tensor // 2, tensor % 2

    norm_rows = norm_params.shape[1]

    positions = jnp.arange(cell, dtype=jnp.int32)
    key_valid = (positions[None, :] < lengths[:, None]) & (
        (key_mask == 1) | (positions[None, :] == 0)
    )
    bias = jnp.where(key_valid, 0.0, -1e30).astype(F32)
    bias = jnp.where(side == 0, bias, bias[::-1])
    bias = jnp.where(core == 0, bias, jnp.roll(bias, own, axis=1))
    bias_near, bias_far = [jnp.broadcast_to(row, (8, cell)) for row in bias]

    slow, _ = dp_split(lax.axis_size("dp"))
    odds, evens = list(range(1, slow, 2)), list(range(2, slow, 2))
    qkv_width = 3 * heads * HD
    head = own // 4
    first_low = pack_first(qkv_weight.transpose(1, 0, 2), out_weight)
    first = {k: high_swap(first_low, k) for k in odds}
    first_own = spread(first_low)
    top = own // 4
    side_top = side_swap(tokens[:top])
    mate_tokens = core_swap(tokens)
    norm_low, mate_tokens = tie(norm_params.astype(BF16), mate_tokens)
    norm_low = gather_small(norm_low)
    up_low, down_low = up_weight.astype(BF16), down_weight.astype(BF16)
    first, first_own, side_top, tokens, up_low, down_low = tie(
        first, first_own, side_top, tokens, up_low, down_low
    )
    for k in evens:
        first[k] = high_swap(first[k ^ 1], 1)
    first_lines = {k: spread(first[k]) for k in odds}
    side_rest = side_swap(tokens[top:])
    top_mate = core_swap(side_top)
    first, first_lines, up_low, down_low, cotangent, side_rest, top_mate, norm_low = tie(
        first, first_lines, up_low, down_low, cotangent, side_rest, top_mate, norm_low
    )
    for k in evens:
        first_lines[k] = spread(first[k])
    rest_mate = core_swap(side_rest)
    up = {k: high_swap(up_low, k) for k in odds}
    norm_values = jnp.moveaxis(norm_low, 0, 1).reshape(4, width).astype(F32)
    one_near = norm_tokens([tokens, mate_tokens], norm_values[:2])
    one_far = norm_tokens([side_top, side_rest, top_mate, rest_mate], norm_values[:2])
    cot_side = side_swap(cotangent)
    first_lines, one_far, one_near, up_low = tie(first_lines, one_far, one_near, up_low)
    up_own = spread(up_low)[1:]

    qkv_full, out_full = assemble(
        sum([entries(k, line) for k, line in first_lines.items()], entries(0, first_own)),
        qkv_width,
    )
    qkv_far, ctx_far, lse_far = attend(one_far, qkv_full, bias_far, heads)
    ctx_far, up, up_own, cot_side, down_low = tie(ctx_far, up, up_own, cot_side, down_low)
    for k in evens:
        up[k] = high_swap(up[k ^ 1], 1)
    up_others = spread(jnp.stack([up[k] for k in odds] + [down_low]))[1:]
    down = {k: high_swap(down_low, k) for k in odds}
    far_sum = cores_sum(ctx_far, out_full).astype(BF16)
    far_sum, one_near, qkv_full = tie(far_sum, one_near, qkv_full)
    out_far = side_swap(far_sum)
    qkv_near, ctx_near, lse_near = attend(one_near, qkv_full, bias_near, heads)
    ctx_near, out_far, up, up_others, down, cotangent, cot_side = tie(
        ctx_near, out_far, up, up_others, down, cotangent, cot_side
    )
    for k in evens:
        down[k] = high_swap(down[k ^ 1], 1)
    up_even = [spread(up[k])[1:] for k in evens]
    out_near = cores_sum(ctx_near, out_full)
    stream_in = tokens.astype(F32)
    residual = stream_in + (out_near + out_far.astype(F32))

    ln_two, normed_two, inverse_two = layer_norm_parts(residual, norm_values[2], norm_values[3])
    ln_two = ln_two.astype(BF16)
    ln_two, up_even, down = tie(ln_two, up_even, down)
    two_mate = core_swap(ln_two)
    two_side = side_swap(ln_two)
    places = odds + evens
    down_line = jnp.stack([down[k] for k in places])
    down_others = spread(down_line)[1:]
    grad_near = with_mate(cotangent)
    grad_far = with_mate(cot_side)
    two_near = join([ln_two, two_mate])
    two_near, grad_near, grad_far = tie(two_near, grad_near, grad_far)
    (up_full,) = assemble(
        entries(0, [up_low, *up_own])
        + joined_entries(odds, [up[k] for k in odds], up_others)
        + [
            entry
            for k, line in zip(evens, up_even, strict=True)
            for entry in entries(k, [up[k], *line])
        ]
    )
    hid_near, slope_near = gelu_parts(dot(two_near, up_full))
    hid_near, down_line, down_others, two_side = tie(hid_near, down_line, down_others, two_side)
    (down_full,) = assemble(
        [(0, 0, down_low, None)]
        + [(0, j + 1, other, len(odds)) for j, other in enumerate(up_others)]
        + [
            entry
            for n, k in enumerate(places)
            for entry in [(k, 0, down_line, n)]
            + [(k, j + 1, other, n) for j, other in enumerate(down_others)]
        ]
    )
    two_far = with_mate(two_side)
    pre_near = (dot(grad_near, down_full, NT) * slope_near.astype(F32)).astype(BF16)
    two_far, pre_near = tie(two_far, pre_near)
    hid_far, slope_far = gelu_parts(dot(two_far, up_full))
    pre_far = (dot(grad_far, down_full, NT) * slope_far.astype(F32)).astype(BF16)
    far_sum = cores_sum(pre_far, up_full, NT).astype(BF16)
    far_sum, pre_near, pre_far, hid_near, hid_far = tie(
        far_sum, pre_near, pre_far, hid_near, hid_far
    )
    back_far = side_swap(far_sum)
    back_near = cores_sum(pre_near, up_full, NT)
    back_near, hid_near, hid_far, grad_near, grad_far = tie(
        back_near, hid_near, hid_far, grad_near, grad_far
    )
    heavy, light = relay_ks()
    order = heavy + light
    grad_down = dot(join([hid_near, hid_far]), join([grad_near, grad_far]), TN).astype(BF16)
    grad_down, hid_near, hid_far = tie(grad_down, hid_near, hid_far)
    down_received = [scatter_send(grad_down, heavy)]
    last_terms = [dot(v[own:], down_full).astype(BF16) for v in (hid_far, hid_near)]
    last_terms, pre_near, pre_far = tie(last_terms, pre_near, pre_far)
    grad_up = weight_grad([two_near, two_far], [pre_near, pre_far])
    last_terms, grad_down, back_far, grad_up, down_received = tie(
        last_terms, grad_down, back_far, grad_up, down_received
    )
    grad_ln_two = back_near + back_far.astype(F32)
    grad_residual = cotangent.astype(F32) + layer_norm_back(
        grad_ln_two, normed_two, inverse_two, norm_values[2]
    )
    gain_two = jnp.sum(grad_ln_two * normed_two, axis=0)
    shift_two = jnp.sum(grad_ln_two, axis=0)

    res_low = grad_residual.astype(BF16)
    res_side = side_swap(res_low)
    res_mate = core_swap(res_low)
    last_mates = [core_swap(v) for v in last_terms]
    down_lines = scatter_lines(grad_down, heavy, down_received[0])
    res_mate, last_mates, down_lines = tie(res_mate, last_mates, down_lines)
    down_got = relay_send(down_lines)
    up_received = [scatter_send(grad_up, heavy)]
    dqkv_near = attend_back(
        qkv_near, bias_near, ctx_near, lse_near, res_low, res_mate, out_full, heads
    )
    dqkv_near, res_side, up_received, grad_up, down_got, grad_down, last_mates, hid_far = tie(
        dqkv_near, res_side, up_received, grad_up, down_got, grad_down, last_mates, hid_far
    )
    down_received.append(scatter_send(grad_down, light))
    res_side_mate = core_swap(res_side)
    up_lines = scatter_lines(grad_up, heavy, up_received[0])
    last_far = own_sum(hid_far, down_full, last_mates[0]).astype(BF16)
    grad_out = weight_grad(
        [ctx_near, ctx_far], [res_low, res_mate, res_side, res_side_mate], ctx_near.shape[1]
    )
    grad_out, last_far, grad_down, down_received[1] = tie(
        grad_out, last_far, grad_down, down_received[1]
    )
    down_lines.update(scatter_lines(grad_down, light, down_received[1]))
    res_side_mate, grad_out, down_lines, up_lines, last_far = tie(
        res_side_mate, grad_out, down_lines, up_lines, last_far
    )
    up_received.append(scatter_send(grad_up, light))
    out_received = scatter_send(grad_out, order)
    down_parts = relay_last(down_lines, down_got)
    up_got = relay_send(up_lines)
    last_side = side_swap(last_far)
    dqkv_far = attend_back(
        qkv_far, bias_far, ctx_far, lse_far, res_side, res_side_mate, out_full, heads
    )
    dqkv_far, up_got, up_received, grad_up, down_parts, grad_out, out_received, last_side = tie(
        dqkv_far, up_got, up_received, grad_up, down_parts, grad_out, out_received, last_side
    )

    up_lines.update(scatter_lines(grad_up, light, up_received[1]))
    out_lines = scatter_lines(grad_out, order, out_received)
    dqkv_far, dqkv_near, up_lines, out_lines = tie(dqkv_far, dqkv_near, up_lines, out_lines)
    up_parts = relay_last(up_lines, up_got)
    out_got = relay_send(out_lines)
    grad_qkv = dot(join([one_near, one_far]), join([dqkv_near, dqkv_far]), TN).astype(BF16)
    grad_qkv, dqkv_far, dqkv_near = tie(rows_first(grad_qkv), dqkv_far, dqkv_near)
    received = [scatter_send(grad_qkv, heavy)]
    first_mates = [mates_part(v, qkv_full, NT) for v in (dqkv_far, dqkv_near)]
    far_sum = own_sum(dqkv_far, qkv_full, first_mates[0], NT).astype(BF16)
    far_sum, first_mates, grad_qkv, dqkv_near, hid_near = tie(
        far_sum, first_mates, grad_qkv, dqkv_near, hid_near
    )
    first_far = side_swap(far_sum)
    received.append(scatter_send(grad_qkv, light))
    first_near = own_sum(dqkv_near, qkv_full, first_mates[1], NT)
    first_near, received[0], grad_qkv, hid_near = tie(first_near, received[0], grad_qkv, hid_near)
    qkv_lines = scatter_lines(grad_qkv, heavy, received[0])
    qkv_got = relay_send(qkv_lines)
    last_near = own_sum(hid_near, down_full, last_mates[1])
    layer_out = (residual + (last_near + last_side.astype(F32))).astype(BF16)
    (
        received[1], qkv_got, qkv_lines, out_got, out_lines, layer_out, up_parts, down_parts,
        grad_qkv,
    ) = tie(
        received[1], qkv_got, qkv_lines, out_got, out_lines, layer_out, up_parts, down_parts,
        grad_qkv,
    )
    qkv_lines.update(scatter_lines(grad_qkv, light, received[1]))
    qkv_parts = relay_last(qkv_lines, qkv_got)
    out_parts = relay_last(out_lines, out_got)
    summed_up, summed_down = parts_sum(up_parts), parts_sum(down_parts)
    early_squares = jnp.sum(summed_up * summed_up) + jnp.sum(summed_down * summed_down)

    input_grad, sums_one = first_back(tokens, first_near, first_far, grad_residual, norm_values)
    rows_two = jnp.stack([gain_two, shift_two])
    qkv_parts, sums_one, input_grad, early_squares = tie(
        qkv_parts, sums_one, input_grad, early_squares
    )
    packed = squares_packed(sums_one, rows_two, early_squares, [qkv_parts, out_parts])
    packed = sum_all(packed)
    summed_norm = lax.dynamic_slice_in_dim(packed, dp * norm_rows, norm_rows, 1)
    grad_norm, shift_grad, results = adam_all(
        packed,
        [
            (*[v.transpose(1, 0, 2) for v in (qkv_weight, qkv_first, qkv_second)], qkv_parts, RATE_QKV),
            (out_weight, out_first, out_second, out_parts, RATE_OUT),
            (up_weight, up_first, up_second, up_parts, RATE_UP),
            (down_weight, down_first, down_second, down_parts, RATE_DOWN),
            (norm_params, norm_first, norm_second, [summed_norm], RATE_NORM),
        ],
    )
    grad_norm, shift_grad = grad_norm[0, 0], shift_grad[0]
    qkv_new, qkv_one, qkv_two = [v.transpose(1, 0, 2) for v in results[0]]
    out_new, out_one, out_two = results[1]
    up_new, up_one, up_two = results[2]
    down_new, down_one, down_two = results[3]
    norm_new, norm_one, norm_two = results[4]
    return (
        layer_out,
        input_grad,
        grad_norm,
        qkv_new,
        qkv_one,
        qkv_two,
        out_new,
        out_one,
        out_two,
        up_new,
        up_one,
        up_two,
        down_new,
        down_one,
        down_two,
        norm_new,
        norm_one,
        norm_two,
        shift_grad,
    )


def solution(mesh):
    tokens = P(("dp", "tensor"), None)
    columns = P("dp", None, "tensor")
    rows = P(("tensor", "dp"), None)
    both = P("dp", "tensor")
    norms = P(None, "dp")
    return jax.shard_map(
        on_device,
        mesh=mesh,
        in_specs=(tokens, tokens, P("dp"), P("dp", None), columns, rows, both, rows, norms)
        + (columns,) * 2
        + (rows,) * 2
        + (both,) * 2
        + (rows,) * 2
        + (norms,) * 2,
        out_specs=(tokens, tokens, P())
        + (columns,) * 3
        + (rows,) * 3
        + (both,) * 3
        + (rows,) * 3
        + (norms,) * 3
        + (P("dp"),),
        check_vma=False,
    )
```

profile of v0, /device:TPU:0, one launch (start us, length us, event | category | flops | bytes accessed | tf_op | source)
XLA Modules:
  0.0 427.9 jit_solution(6086340767169795079)
XLA Ops:
  3.4 2.7 collective-permute-start
  6.1 2.5 collective-permute-start.1
  15.6 4.3 %collective-permute-done.10 = bf16[1,4,160]{2,1,0:T(4,128)(2,1)S(1)} collective-permute-done((bf16[1,4,160]{2,1,0:T(4,128)(2,1)S(1)}, bf16[1,4,160]{2,1,0:T(4,128)(2,1)S(1)}, u32[]{:S(2)}, u32[]{:S(2)}) %collective-permute-start.10) | collective-permute-done | bytes 1312 | tf_op jit(solution)/shard_map/ppermute | solution.py:185
  20.7 3.7 collective-permute-done.11
  24.4 3.6 collective-permute-start.12
  28.0 1.9 convert_element_type.328.refs_0_
  39.0 3.2 collective-permute-done.4.refs_4_
  42.3 10.2 %collective-permute-done.5.refs_3_ = bf16[160,1280]{1,0:T(8,128)(2,1)S(1)} collective-permute-done((bf16[160,1280]{1,0:T(8,128)(2,1)S(1)}, bf16[160,1280]{1,0:T(8,128)(2,1)S(1)}, u32[]{:S(2)}, u32[]{:S(2)}) %collective-permute-start.5) | collective-permute-done | bytes 409632 | tf_op jit(solution)/shard_map/ppermute | solution.py:185
  54.0 3.7 collective-permute-done.7.refs_1_
  64.5 1.9 norm_tokens.3.one_ref
  66.5 4.5 %norm_tokens.2.one_ref = bf16[1024,1280]{1,0:T(8,128)(2,1)S(1)} custom-call(bf16[128,1280]{1,0:T(8,128)(2,1)} %collective-permute-done.3.refs_0_, bf16[384,1280]{1,0:T(8,128)(2,1)} %collective-permute-done.7.refs_1_, bf16[128,1280]{1,0:T(8,128)(2,1)S(1)} %copy-done.66, bf16[384,1280]{1,0:T(8,128)(2,1)} %collective-permute-done.14.refs_3_, ...), custom_call_target="tpu_custom_call" | custom-call | bytes 1 | tf_op jit(solution)/shard_map/norm_tokens/pallas_call | solution.py:427
  73.2 3.1 assemble.3
  77.9 12.7 %attend.2 = (bf16[1024,960]{1,0:T(8,128)(2,1)S(1)}, bf16[1024,320]{1,0:T(8,128)(2,1)S(1)}, f32[1024,128]{1,0:T(8,128)S(1)}) custom-call(bf16[1024,1280]{1,0:T(8,128)(2,1)S(1)} %norm_tokens.2.one_ref, bf16[1280,960]{1,0:T(8,128)(2,1)} %bitcast.49, f32[8,1024]{1,0:T(8,128)S(1)} %broadcast_in_dim.27.bias_ref), custom_call_target="tpu_custom_call" | custom-call | bytes 1 | tf_op jit(solution)/shard_map/attend/pallas_call | solution.py:90
  91.6 3.0 collective-permute-done.19
  101.8 12.7 %attend.3 = (bf16[1024,960]{1,0:T(8,128)(2,1)S(1)}, bf16[1024,320]{1,0:T(8,128)(2,1)S(1)}, f32[1024,128]{1,0:T(8,128)S(1)}) custom-call(bf16[1024,1280]{1,0:T(8,128)(2,1)S(1)} %norm_tokens.3.one_ref, bf16[1280,960]{1,0:T(8,128)(2,1)} %bitcast.50, f32[8,1024]{1,0:T(8,128)S(1)} %broadcast_in_dim.28.bias_ref), custom_call_target="tpu_custom_call" | custom-call | bytes 1 | tf_op jit(solution)/shard_map/attend/pallas_call | solution.py:90
  115.3 4.6 %collective-permute-done.23 = bf16[160,1280]{1,0:T(8,128)(2,1)S(1)} collective-permute-done((bf16[160,1280]{1,0:T(8,128)(2,1)}, bf16[160,1280]{1,0:T(8,128)(2,1)S(1)}, u32[]{:S(2)}, u32[]{:S(2)}) %collective-permute-start.23) | collective-permute-done | bytes 409632 | tf_op jit(solution)/shard_map/ppermute | solution.py:185
  120.0 7.3 %collective-permute-done.24 = bf16[160,1280]{1,0:T(8,128)(2,1)S(1)} collective-permute-done((bf16[160,1280]{1,0:T(8,128)(2,1)}, bf16[160,1280]{1,0:T(8,128)(2,1)S(1)}, u32[]{:S(2)}, u32[]{:S(2)}) %collective-permute-start.24) | collective-permute-done | bytes 409632 | tf_op jit(solution)/shard_map/ppermute | solution.py:185
  127.3 2.3 convolution_convert_fusion.7
  133.0 2.9 fusion.67
  137.4 4.6 %collective-permute-done.26.refs_7_ = bf16[160,1280]{1,0:T(8,128)(2,1)S(1)} collective-permute-done((bf16[160,1280]{1,0:T(8,128)(2,1)}, bf16[160,1280]{1,0:T(8,128)(2,1)S(1)}, u32[]{:S(2)}, u32[]{:S(2)}) %collective-permute-start.26) | collective-permute-done | bytes 409632 | tf_op jit(solution)/shard_map/ppermute | solution.py:185
  145.6 2.5 pad_maximum_fusion.2
  148.2 2.3 assemble.4
  150.7 5.2 %multiply_convert_fusion.3 = (bf16[1024,1280]{1,0:T(8,128)(2,1)}, f32[1024,1280]{1,0:T(8,128)S(1)}) fusion(bf16[1024,1280]{1,0:T(8,128)(2,1)S(1)} %pad_maximum_fusion.refs_0_, bf16[1280,1280]{1,0:T(8,128)(2,1)S(1)} %bitcast.62), kind=kOutput, calls=%fused_computation.27 | convolution fusion | flops 3361996800 | bytes 13762560 | tf_op jit(solution)/shard_map/dot_general | solution.py:35
  155.9 17.7 %collective-permute-done.31.refs_3_.refs_5_.refs_7_ = bf16[3,160,1280]{2,1,0:T(8,128)(2,1)S(1)} collective-permute-done((bf16[3,160,1280]{2,1,0:T(8,128)(2,1)S(1)}, bf16[3,160,1280]{2,1,0:T(8,128)(2,1)S(1)}, u32[]{:S(2)}, u32[]{:S(2)}) %collective-permute-start.31) | collective-permute-done | bytes 1228832 | tf_op jit(solution)/shard_map/ppermute | solution.py:185
  173.9 2.3 assemble.5
  176.2 5.5 %multiply_convert_fusion.2.refs_2_ = bf16[1024,1280]{1,0:T(8,128)(2,1)S(1)} fusion(bf16[1024,1280]{1,0:T(8,128)(2,1)S(1)} %pad_maximum_fusion.1, bf16[1280,1280]{1,0:T(8,128)(2,1)S(1)} %bitcast.56, f32[1024,1280]{1,0:T(8,128)S(1)} %get-tuple-element.440), kind=kOutput, calls=%fused_computation.26 | convolution fusion | flops 3371171840 | bytes 13762560 | tf_op jit(solution)/shard_map/dot_general | solution.py:35
  181.9 5.1 %multiply_convert_fusion = (bf16[1024,1280]{1,0:T(8,128)(2,1)}, f32[1024,1280]{1,0:T(8,128)S(1)}) fusion(bf16[1024,1280]{1,0:T(8,128)(2,1)S(1)} %pad_maximum_fusion.3.refs_1_, bf16[1280,1280]{1,0:T(8,128)(2,1)S(1)} %bitcast.63), kind=kOutput, calls=%fused_computation.23 | convolution fusion | flops 3361996800 | bytes 13762560 | tf_op jit(solution)/shard_map/dot_general | solution.py:35
  187.0 5.7 %multiply_convert_fusion.1.refs_3_ = bf16[1024,1280]{1,0:T(8,128)(2,1)S(1)} fusion(bf16[1024,1280]{1,0:T(8,128)(2,1)S(1)} %pad_maximum_fusion.2, bf16[1280,1280]{1,0:T(8,128)(2,1)S(1)} %bitcast.57, f32[1024,1280]{1,0:T(8,128)S(1)} %get-tuple-element.442), kind=kOutput, calls=%fused_computation.24 | convolution fusion | flops 3371171840 | bytes 13762560 | tf_op jit(solution)/shard_map/dot_general | solution.py:35
  192.7 1.9 convolution_convert_fusion.6
  195.1 2.7 collective-permute-done.34
  197.8 3.0 add_convert_fusion.1
  200.8 3.0 convolution_convert_fusion.5
  207.2 4.6 %convert_add_fusion.1 = f32[512,1280]{1,0:T(8,128)S(1)} fusion(bf16[512,1280]{1,0:T(8,128)(2,1)} %collective-permute-done.35, bf16[1280,1280]{1,0:T(8,128)(2,1)} %bitcast.67, bf16[1024,1280]{1,0:T(8,128)(2,1)} %copy-done.30), kind=kOutput, calls=%fused_computation.61 | convolution fusion | flops 1679032320 | bytes 8519680 | tf_op jit(solution)/shard_map/dot_general | solution.py:35
  211.8 7.4 %convolution_convert_fusion = bf16[1280,1280]{1,0:T(8,128)(2,1)S(1)} fusion(bf16[1024,1280]{1,0:T(8,128)(2,1)S(1)} %copy-done.96, bf16[1024,1280]{1,0:T(8,128)(2,1)S(1)} %copy-done.98, bf16[1024,1280]{1,0:T(8,128)(2,1)S(1)} %copy-done.82, bf16[1024,1280]{1,0:T(8,128)(2,1)S(1)} %copy-done.80), kind=kOutput, calls=%fused_computation.2 | convolution fusion | flops 6733496320 | bytes 13762560 | tf_op jit(solution)/shard_map/dot_general | solution.py:35
  222.6 2.9 convolution_convert_fusion.4
  225.6 2.9 convolution_convert_fusion.3
  229.4 8.1 %weight_grad.2 = bf16[1280,1280]{1,0:T(8,128)(2,1)S(1)} custom-call(bf16[1024,1280]{1,0:T(8,128)(2,1)S(1)} %copy-done.10, bf16[1024,1280]{1,0:T(8,128)(2,1)S(1)} %pad_maximum_fusion.3.refs_1_, bf16[1024,1280]{1,0:T(8,128)(2,1)S(1)} %copy-done.31, bf16[1024,1280]{1,0:T(8,128)(2,1)S(1)} %copy-done.33), custom_call_target="tpu_custom_call" | custom-call | bytes 1 | tf_op jit(solution)/shard_map/weight_grad/pallas_call | solution.py:453
  237.5 3.5 collective-permute-done.37
  242.8 2.7 fusion.64
  253.9 19.0 %attend_back.2 = bf16[1024,960]{1,0:T(8,128)(2,1)} custom-call(bf16[1024,960]{1,0:T(8,128)(2,1)} %copy-done.35, f32[8,1024]{1,0:T(8,128)S(1)} %broadcast_in_dim.28.bias_ref, bf16[1024,320]{1,0:T(8,128)(2,1)S(1)} %copy-done.12, f32[1024,128]{1,0:T(8,128)S(1)} %copy-done.47, bf16[512,1280]{1,0:T(8,128)(2,1)S(1)} %get-tuple-element.399.own_ref.refs_2_, ...), custom_call_target="tpu_custom_call" | custom-call | bytes 1 | tf_op jit(solution)/shard_map/attend_back/pallas_call | solution.py:169
  273.0 4.4 %collective-permute-done.41.refs_4_.own_ref = bf16[512,1280]{1,0:T(8,128)(2,1)} collective-permute-done((bf16[512,1280]{1,0:T(8,128)(2,1)S(1)}, bf16[512,1280]{1,0:T(8,128)(2,1)}, u32[]{:S(2)}, u32[]{:S(2)}) %collective-permute-start.41) | collective-permute-done | bytes 1310752 | tf_op jit(solution)/shard_map/ppermute | solution.py:185
  282.0 4.2 fusion.33
  286.3 4.1 weight_grad.3
  290.4 8.3 %collective-permute-done.45 = bf16[320,1280]{1,0:T(8,128)(2,1)S(1)} collective-permute-done((bf16[320,1280]{1,0:T(8,128)(2,1)S(1)}, bf16[320,1280]{1,0:T(8,128)(2,1)S(1)}, u32[]{:S(2)}, u32[]{:S(2)}) %collective-permute-start.45) | collective-permute-done | bytes 819232 | tf_op jit(solution)/shard_map/ppermute | solution.py:185
  302.4 1.8 add_convert_fusion.6
  304.2 2.2 collective-permute-start.48
  309.5 19.2 %attend_back.3 = bf16[1024,960]{1,0:T(8,128)(2,1)} custom-call(bf16[1024,960]{1,0:T(8,128)(2,1)} %copy-done.34, f32[8,1024]{1,0:T(8,128)S(1)} %broadcast_in_dim.27.bias_ref, bf16[1024,320]{1,0:T(8,128)(2,1)S(1)} %copy-done.15, f32[1024,128]{1,0:T(8,128)S(1)} %copy-done.45, bf16[512,1280]{1,0:T(8,128)(2,1)} %collective-permute-done.41.refs_4_.own_ref, ...), custom_call_target="tpu_custom_call" | custom-call | bytes 1 | tf_op jit(solution)/shard_map/attend_back/pallas_call | solution.py:169
  333.9 7.8 %fusion.23 = bf16[1280,960]{1,0:T(8,128)(2,1)S(1)} fusion(bf16[1024,960]{1,0:T(8,128)(2,1)} %attend_back.3, bf16[1024,960]{1,0:T(8,128)(2,1)S(1)} %copy-done.83, bf16[1024,1280]{1,0:T(8,128)(2,1)S(1)} %copy-done.8, bf16[1024,1280]{1,0:T(8,128)(2,1)S(1)} %copy-done.6), kind=kOutput, calls=%fused_computation.32 | convolution fusion | flops 5052743680 | bytes 11632640 | tf_op jit(solution)/shard_map/dot_general | solution.py:35
  350.8 2.2 collective-permute-start.57
  353.1 2.7 add_convert_fusion
  356.9 3.1 convolution_add_fusion.2.near_ref
  360.0 3.3 collective-permute-done.54
  363.6 1.8 collective-permute-start.55
  366.9 4.7 %fusion.31 = bf16[512,1280]{1,0:T(8,128)(2,1)} fusion(f32[512,1280]{1,0:T(8,128)S(1)} %copy-done.70, bf16[1280,1280]{1,0:T(8,128)(2,1)S(1)} %bitcast.61, bf16[512,1280]{1,0:T(8,128)(2,1)} %collective-permute-done.50, bf16[512,1280]{1,0:T(8,128)(2,1)} %collective-permute-done.40, bf16[1024,1280]{1,0:T(8,128)(2,1)S(1)} %copy-done.99), kind=kOutput, calls=%fused_computation.41 | convolution fusion | flops 1681653760 | bytes 11141120 | tf_op jit(solution)/shard_map/dot_general | solution.py:35
  371.6 4.8 %collective-permute-done.53 = bf16[320,960]{1,0:T(8,128)(2,1)S(1)} collective-permute-done((bf16[320,960]{1,0:T(8,128)(2,1)S(1)}, bf16[320,960]{1,0:T(8,128)(2,1)S(1)}, u32[]{:S(2)}, u32[]{:S(2)}) %collective-permute-start.53) | collective-permute-done | bytes 614432 | tf_op jit(solution)/shard_map/ppermute | solution.py:185
  376.4 2.2 collective-permute-done.55
  378.9 2.2 collective-permute-start.58
  383.7 1.8 multiply_reduce_fusion.4
  386.9 7.5 %collective-permute-done.59.far_ref = bf16[512,1280]{1,0:T(8,128)(2,1)} collective-permute-done((bf16[512,1280]{1,0:T(8,128)(2,1)}, bf16[512,1280]{1,0:T(8,128)(2,1)}, u32[]{:S(2)}, u32[]{:S(2)}) %collective-permute-start.59) | collective-permute-done | bytes 1310752 | tf_op jit(solution)/shard_map/ppermute | solution.py:185
  394.4 6.2 %first_back.1 = (bf16[512,1280]{1,0:T(8,128)(2,1)}, f32[16,1280]{1,0:T(8,128)}) custom-call(bf16[512,1280]{1,0:T(8,128)(2,1)} %tokens_ref, f32[512,1280]{1,0:T(8,128)} %convolution_add_fusion.2.near_ref, bf16[512,1280]{1,0:T(8,128)(2,1)} %collective-permute-done.59.far_ref, f32[512,1280]{1,0:T(8,128)} %get-tuple-element.400.res_ref, ...), custom_call_target="tpu_custom_call" | custom-call | bytes 1 | tf_op jit(solution)/shard_map/first_back/pallas_call | solution.py:535
  404.4 1.9 collective-permute-start.64
  407.2 2.1 collective-permute-done.64
  415.0 2.0 collective-permute-done.67
  417.7 10.0 %adam_all.1 = (f32[3,160,320]{2,1,0:T(8,128)}, f32[3,160,320]{2,1,0:T(8,128)}, f32[3,160,320]{2,1,0:T(8,128)}, f32[40,1280]{1,0:T(8,128)}, f32[40,1280]{1,0:T(8,...) custom-call(f32[4,1408]{1,0:T(4,128)} %copy-done.91, ...), custom_call_target="tpu_custom_call" | custom-call | tf_op jit(solution)/shard_map/adam_all/pallas_call | solution.py:616
  (398 shorter events, 110.2 us)
Async XLA Ops:
  0.7 10.2 %collective-permute-start.9 = (bf16[512,1280]{1,0:T(8,128)(2,1)}, bf16[512,1280]{1,0:T(8,128)(2,1)S(1)}, u32[]{:S(2)}, u32[]{:S(2)}) collective-permute-start(bf16[512,1280]{1,0:T(8,128)(2,1)} %tokens_ref), channel_id=1, source_target_pairs={{0,1},{1,0},{2,3},{3,2},{4,5},{5,4},{6,7},{7,6},{8,9},{9,8},{10,11... | collective-permute-start | bytes 3932168 | tf_op jit(solution)/shard_map/ppermute | solution.py:185
  3.4 27.8 %collective-permute-start = (bf16[160,1280]{1,0:T(8,128)(2,1)S(1)}, bf16[160,1280]{1,0:T(8,128)(2,1)S(1)}, u32[]{:S(2)}, u32[]{:S(2)}) collective-permute-start(bf16[160,1280]{1,0:T(8,128)(2,1)S(1)} %pack_first.1.refs_0_), channel_id=1, source_target_pairs={{0,8},{4,12},{8,0},{12,4},{16,24},{20,28},{24,16},{28,20},{1,9},{5... | collective-permute-start | bytes 1228808 | tf_op jit(solution)/shard_map/ppermute | solution.py:185
  6.1 25.1 %collective-permute-start.1 = (bf16[160,1280]{1,0:T(8,128)(2,1)S(1)}, bf16[160,1280]{1,0:T(8,128)(2,1)S(1)}, u32[]{:S(2)}, u32[]{:S(2)}) collective-permute-start(bf16[160,1280]{1,0:T(8,128)(2,1)S(1)} %pack_first.1.refs_0_), channel_id=1, source_target_pairs={{0,24},{4,28},{8,16},{12,20},{16,8},{20,12},{24,0},{28,4},{1,25},{... | collective-permute-start | bytes 1228808 | tf_op jit(solution)/shard_map/ppermute | solution.py:185
  8.6 22.6 %collective-permute-start.2 = (bf16[160,1280]{1,0:T(8,128)(2,1)S(1)}, bf16[160,1280]{1,0:T(8,128)(2,1)S(1)}, u32[]{:S(2)}, u32[]{:S(2)}) collective-permute-start(bf16[160,1280]{1,0:T(8,128)(2,1)S(1)} %pack_first.1.refs_0_), channel_id=1, source_target_pairs={{0,4},{4,0},{8,12},{12,8},{16,20},{20,16},{24,28},{28,24},{1,5},{5... | collective-permute-start | bytes 1228808 | tf_op jit(solution)/shard_map/ppermute | solution.py:185
  11.9 8.0 %collective-permute-start.10 = (bf16[1,4,160]{2,1,0:T(4,128)(2,1)S(1)}, bf16[1,4,160]{2,1,0:T(4,128)(2,1)S(1)}, u32[]{:S(2)}, u32[]{:S(2)}) collective-permute-start(bf16[1,4,160]{2,1,0:T(4,128)(2,1)S(1)} %bitcast.76), channel_id=1, source_target_pairs={{0,4},{4,0},{8,12},{12,8},{16,20},{20,16},{24,28},{28,24},{1,5},{5... | collective-permute-start | bytes 3848 | tf_op jit(solution)/shard_map/ppermute | solution.py:185
  14.1 17.1 %collective-permute-start.3 = (bf16[128,1280]{1,0:T(8,128)(2,1)}, bf16[128,1280]{1,0:T(8,128)(2,1)}, u32[]{:S(2)}, u32[]{:S(2)}) collective-permute-start(bf16[128,1280]{1,0:T(8,128)(2,1)} %slice.150), channel_id=1, source_target_pairs={{0,2},{1,3},{2,0},{3,1},{4,6},{5,7},{6,4},{7,5},{8,10},{9,11},{10,... | collective-permute-start | bytes 983048 | tf_op jit(solution)/shard_map/ppermute | solution.py:185
  19.9 4.5 %collective-permute-start.11 = (bf16[2,4,160]{2,1,0:T(4,128)(2,1)S(1)}, bf16[2,4,160]{2,1,0:T(4,128)(2,1)S(1)}, u32[]{:S(2)}, u32[]{:S(2)}) collective-permute-start(bf16[2,4,160]{2,1,0:T(4,128)(2,1)S(1)} %pad_maximum_fusion.20), channel_id=1, source_target_pairs={{0,8},{4,12},{8,0},{12,4},{16,24},{20,28},{24,16},{28,20},{1,9},{5... | collective-permute-start | bytes 7688 | tf_op jit(solution)/shard_map/ppermute | solution.py:185
  24.4 12.1 %collective-permute-start.12 = (bf16[4,4,160]{2,1,0:T(4,128)(2,1)S(1)}, bf16[4,4,160]{2,1,0:T(4,128)(2,1)S(1)}, u32[]{:S(2)}, u32[]{:S(2)}) collective-permute-start(bf16[4,4,160]{2,1,0:T(4,128)(2,1)S(1)} %pad_maximum_fusion.19), channel_id=1, source_target_pairs={{0,16},{4,20},{8,24},{12,28},{16,0},{20,4},{24,8},{28,12},{1,17},{... | collective-permute-start | bytes 15368 | tf_op jit(solution)/shard_map/ppermute | solution.py:185
  31.2 11.0 %collective-permute-start.4 = (bf16[160,1280]{1,0:T(8,128)(2,1)S(1)}, bf16[160,1280]{1,0:T(8,128)(2,1)S(1)}, u32[]{:S(2)}, u32[]{:S(2)}) collective-permute-start(bf16[160,1280]{1,0:T(8,128)(2,1)S(1)} %collective-permute-done.1.refs_6_), channel_id=1, source_target_pairs={{0,8},{4,12},{8,0},{12,4},{16,24},{20,28},{24,16},{28,20},{1,9},{5... | collective-permute-start | bytes 1228808 | tf_op jit(solution)/shard_map/ppermute | solution.py:185
  32.8 20.4 %collective-permute-start.6 = (bf16[160,1280]{1,0:T(8,128)(2,1)S(1)}, bf16[160,1280]{1,0:T(8,128)(2,1)S(1)}, u32[]{:S(2)}, u32[]{:S(2)}) collective-permute-start(bf16[160,1280]{1,0:T(8,128)(2,1)S(1)} %collective-permute-done.1.refs_6_), channel_id=1, source_target_pairs={{0,4},{4,0},{8,12},{12,8},{16,20},{20,16},{24,28},{28,24},{1,5},{5... | collective-permute-start | bytes 1228808 | tf_op jit(solution)/shard_map/ppermute | solution.py:185
  34.3 18.2 %collective-permute-start.5 = (bf16[160,1280]{1,0:T(8,128)(2,1)S(1)}, bf16[160,1280]{1,0:T(8,128)(2,1)S(1)}, u32[]{:S(2)}, u32[]{:S(2)}) collective-permute-start(bf16[160,1280]{1,0:T(8,128)(2,1)S(1)} %collective-permute-done.refs_2_), channel_id=1, source_target_pairs={{0,4},{4,0},{8,12},{12,8},{16,20},{20,16},{24,28},{28,24},{1,5},{5... | collective-permute-start | bytes 1228808 | tf_op jit(solution)/shard_map/ppermute | solution.py:185
  34.9 22.8 %collective-permute-start.7 = (bf16[384,1280]{1,0:T(8,128)(2,1)S(1)}, bf16[384,1280]{1,0:T(8,128)(2,1)}, u32[]{:S(2)}, u32[]{:S(2)}) collective-permute-start(bf16[384,1280]{1,0:T(8,128)(2,1)S(1)} %slice.151), channel_id=1, source_target_pairs={{0,2},{1,3},{2,0},{3,1},{4,6},{5,7},{6,4},{7,5},{8,10},{9,11},{10,... | collective-permute-start | bytes 2949128 | tf_op jit(solution)/shard_map/ppermute | solution.py:185
  57.7 8.7 %collective-permute-start.14 = (bf16[384,1280]{1,0:T(8,128)(2,1)}, bf16[384,1280]{1,0:T(8,128)(2,1)}, u32[]{:S(2)}, u32[]{:S(2)}) collective-permute-start(bf16[384,1280]{1,0:T(8,128)(2,1)} %collective-permute-done.7.refs_1_), channel_id=1, source_target_pairs={{0,1},{1,0},{2,3},{3,2},{4,5},{5,4},{6,7},{7,6},{8,9},{9,8},{10,11... | collective-permute-start | bytes 2949128 | tf_op jit(solution)/shard_map/ppermute | solution.py:185
  57.7 32.9 %collective-permute-start.18 = (bf16[512,1280]{1,0:T(8,128)(2,1)}, bf16[512,1280]{1,0:T(8,128)(2,1)}, u32[]{:S(2)}, u32[]{:S(2)}) collective-permute-start(bf16[512,1280]{1,0:T(8,128)(2,1)} %param.20), channel_id=1, source_target_pairs={{0,2},{1,3},{2,0},{3,1},{4,6},{5,7},{6,4},{7,5},{8,10},{9,11},{10,... | collective-permute-start | bytes 3932168 | tf_op jit(solution)/shard_map/ppermute | solution.py:185
  59.7 11.9 %collective-permute-start.13 = (bf16[160,1280]{1,0:T(8,128)(2,1)}, bf16[160,1280]{1,0:T(8,128)(2,1)}, u32[]{:S(2)}, u32[]{:S(2)}) collective-permute-start(bf16[160,1280]{1,0:T(8,128)(2,1)} %copy-done.54), channel_id=1, source_target_pairs={{0,4},{4,0},{8,12},{12,8},{16,20},{20,16},{24,28},{28,24},{1,5},{5... | collective-permute-start | bytes 1228808 | tf_op jit(solution)/shard_map/ppermute | solution.py:185
  61.3 29.3 %collective-permute-start.15 = (bf16[160,1280]{1,0:T(8,128)(2,1)}, bf16[160,1280]{1,0:T(8,128)(2,1)S(1)}, u32[]{:S(2)}, u32[]{:S(2)}) collective-permute-start(bf16[160,1280]{1,0:T(8,128)(2,1)} %convert_element_type.328.refs_0_), channel_id=1, source_target_pairs={{0,8},{4,12},{8,0},{12,4},{16,24},{20,28},{24,16},{28,20},{1,9},{5... | collective-permute-start | bytes 1228808 | tf_op jit(solution)/shard_map/ppermute | solution.py:185
  61.6 29.0 %collective-permute-start.16 = (bf16[160,1280]{1,0:T(8,128)(2,1)}, bf16[160,1280]{1,0:T(8,128)(2,1)}, u32[]{:S(2)}, u32[]{:S(2)}) collective-permute-start(bf16[160,1280]{1,0:T(8,128)(2,1)} %convert_element_type.328.refs_0_), channel_id=1, source_target_pairs={{0,24},{4,28},{8,16},{12,20},{16,8},{20,12},{24,0},{28,4},{1,25},{... | collective-permute-start | bytes 1228808 | tf_op jit(solution)/shard_map/ppermute | solution.py:185
  71.6 19.0 %collective-permute-start.17 = (bf16[160,1280]{1,0:T(8,128)(2,1)}, bf16[160,1280]{1,0:T(8,128)(2,1)S(1)}, u32[]{:S(2)}, u32[]{:S(2)}) collective-permute-start(bf16[160,1280]{1,0:T(8,128)(2,1)} %convert_element_type.328.refs_0_), channel_id=1, source_target_pairs={{0,4},{4,0},{8,12},{12,8},{16,20},{20,16},{24,28},{28,24},{1,5},{5... | collective-permute-start | bytes 1228808 | tf_op jit(solution)/shard_map/ppermute | solution.py:185
  95.7 31.6 %collective-permute-start.20 = (bf16[512,1280]{1,0:T(8,128)(2,1)S(1)}, bf16[512,1280]{1,0:T(8,128)(2,1)S(1)}, u32[]{:S(2)}, u32[]{:S(2)}) collective-permute-start(bf16[512,1280]{1,0:T(8,128)(2,1)S(1)} %fusion.32), channel_id=1, source_target_pairs={{0,2},{1,3},{2,0},{3,1},{4,6},{5,7},{6,4},{7,5},{8,10},{9,11},{10,... | collective-permute-start | bytes 3932168 | tf_op jit(solution)/shard_map/ppermute | solution.py:185
  97.4 29.8 %collective-permute-start.22 = (bf16[3,160,1280]{2,1,0:T(8,128)(2,1)S(1)}, bf16[3,160,1280]{2,1,0:T(8,128)(2,1)S(1)}, u32[]{:S(2)}, u32[]{:S(2)}) collective-permute-start(bf16[3,160,1280]{2,1,0:T(8,128)(2,1)S(1)} %pad_maximum_fusion.4), channel_id=1, source_target_pairs={{0,4},{4,0},{8,12},{12,8},{16,20},{20,16},{24,28},{28,24},{1,5},{5... | collective-permute-start | bytes 3686408 | tf_op jit(solution)/shard_map/ppermute | solution.py:185
  98.6 16.8 %collective-permute-start.21 = (bf16[160,1280]{1,0:T(8,128)(2,1)}, bf16[160,1280]{1,0:T(8,128)(2,1)S(1)}, u32[]{:S(2)}, u32[]{:S(2)}) collective-permute-start(bf16[160,1280]{1,0:T(8,128)(2,1)} %collective-permute-done.16.refs_4_), channel_id=1, source_target_pairs={{0,8},{4,12},{8,0},{12,4},{16,24},{20,28},{24,16},{28,20},{1,9},{5... | collective-permute-start | bytes 1228808 | tf_op jit(solution)/shard_map/ppermute | solution.py:185
  98.9 21.0 %collective-permute-start.23 = (bf16[160,1280]{1,0:T(8,128)(2,1)}, bf16[160,1280]{1,0:T(8,128)(2,1)S(1)}, u32[]{:S(2)}, u32[]{:S(2)}) collective-permute-start(bf16[160,1280]{1,0:T(8,128)(2,1)} %copy-done.18), channel_id=1, source_target_pairs={{0,8},{4,12},{8,0},{12,4},{16,24},{20,28},{24,16},{28,20},{1,9},{5... | collective-permute-start | bytes 1228808 | tf_op jit(solution)/shard_map/ppermute | solution.py:185
  100.6 26.7 %collective-permute-start.24 = (bf16[160,1280]{1,0:T(8,128)(2,1)}, bf16[160,1280]{1,0:T(8,128)(2,1)S(1)}, u32[]{:S(2)}, u32[]{:S(2)}) collective-permute-start(bf16[160,1280]{1,0:T(8,128)(2,1)} %copy-done.18), channel_id=1, source_target_pairs={{0,24},{4,28},{8,16},{12,20},{16,8},{20,12},{24,0},{28,4},{1,25},{... | collective-permute-start | bytes 1228808 | tf_op jit(solution)/shard_map/ppermute | solution.py:185
  129.6 3.4 collective-permute-start.25
  129.9 12.1 %collective-permute-start.26 = (bf16[160,1280]{1,0:T(8,128)(2,1)}, bf16[160,1280]{1,0:T(8,128)(2,1)S(1)}, u32[]{:S(2)}, u32[]{:S(2)}) collective-permute-start(bf16[160,1280]{1,0:T(8,128)(2,1)} %copy-done.62), channel_id=1, source_target_pairs={{0,4},{4,0},{8,12},{12,8},{16,20},{20,16},{24,28},{28,24},{1,5},{5... | collective-permute-start | bytes 1228808 | tf_op jit(solution)/shard_map/ppermute | solution.py:185
  130.9 11.8 %collective-permute-start.27 = (bf16[160,1280]{1,0:T(8,128)(2,1)}, bf16[160,1280]{1,0:T(8,128)(2,1)S(1)}, u32[]{:S(2)}, u32[]{:S(2)}) collective-permute-start(bf16[160,1280]{1,0:T(8,128)(2,1)} %copy-done.89), channel_id=1, source_target_pairs={{0,8},{4,12},{8,0},{12,4},{16,24},{20,28},{24,16},{28,20},{1,9},{5... | collective-permute-start | bytes 1228808 | tf_op jit(solution)/shard_map/ppermute | solution.py:185
  130.9 14.5 %collective-permute-start.29 = (bf16[512,1280]{1,0:T(8,128)(2,1)}, bf16[512,1280]{1,0:T(8,128)(2,1)S(1)}, u32[]{:S(2)}, u32[]{:S(2)}) collective-permute-start(bf16[512,1280]{1,0:T(8,128)(2,1)} %param.20), channel_id=1, source_target_pairs={{0,1},{1,0},{2,3},{3,2},{4,5},{5,4},{6,7},{7,6},{8,9},{9,8},{10,11... | collective-permute-start | bytes 3932168 | tf_op jit(solution)/shard_map/ppermute | solution.py:185
  131.1 14.5 %collective-permute-start.30 = (bf16[512,1280]{1,0:T(8,128)(2,1)}, bf16[512,1280]{1,0:T(8,128)(2,1)S(1)}, u32[]{:S(2)}, u32[]{:S(2)}) collective-permute-start(bf16[512,1280]{1,0:T(8,128)(2,1)} %collective-permute-done.18), channel_id=1, source_target_pairs={{0,1},{1,0},{2,3},{3,2},{4,5},{5,4},{6,7},{7,6},{8,9},{9,8},{10,11... | collective-permute-start | bytes 3932168 | tf_op jit(solution)/shard_map/ppermute | solution.py:185
  142.7 7.8 %collective-permute-start.28 = (bf16[512,1280]{1,0:T(8,128)(2,1)S(1)}, bf16[512,1280]{1,0:T(8,128)(2,1)S(1)}, u32[]{:S(2)}, u32[]{:S(2)}) collective-permute-start(bf16[512,1280]{1,0:T(8,128)(2,1)S(1)} %add_convert_fusion.2), channel_id=1, source_target_pairs={{0,1},{1,0},{2,3},{3,2},{4,5},{5,4},{6,7},{7,6},{8,9},{9,8},{10,11... | collective-permute-start | bytes 3932168 | tf_op jit(solution)/shard_map/ppermute | solution.py:185
  142.7 31.2 %collective-permute-start.32 = (bf16[512,1280]{1,0:T(8,128)(2,1)S(1)}, bf16[512,1280]{1,0:T(8,128)(2,1)S(1)}, u32[]{:S(2)}, u32[]{:S(2)}) collective-permute-start(bf16[512,1280]{1,0:T(8,128)(2,1)S(1)} %add_convert_fusion.2), channel_id=1, source_target_pairs={{0,2},{1,3},{2,0},{3,1},{4,6},{5,7},{6,4},{7,5},{8,10},{9,11},{10,... | collective-permute-start | bytes 3932168 | tf_op jit(solution)/shard_map/ppermute | solution.py:185
  144.3 29.2 %collective-permute-start.31 = (bf16[3,160,1280]{2,1,0:T(8,128)(2,1)S(1)}, bf16[3,160,1280]{2,1,0:T(8,128)(2,1)S(1)}, u32[]{:S(2)}, u32[]{:S(2)}) collective-permute-start(bf16[3,160,1280]{2,1,0:T(8,128)(2,1)S(1)} %pad_maximum_fusion.5.refs_2_.refs_4_.refs_6_), channel_id=1, source_target_pairs={{0,4},{4,0},{8,12},{12,8},{16,20},{20,16},{24,28},{28,24},{1,5},{5... | collective-permute-start | bytes 3686408 | tf_op jit(solution)/shard_map/ppermute | solution.py:185
  173.9 7.8 %collective-permute-start.33 = (bf16[512,1280]{1,0:T(8,128)(2,1)S(1)}, bf16[512,1280]{1,0:T(8,128)(2,1)S(1)}, u32[]{:S(2)}, u32[]{:S(2)}) collective-permute-start(bf16[512,1280]{1,0:T(8,128)(2,1)S(1)} %collective-permute-done.32), channel_id=1, source_target_pairs={{0,1},{1,0},{2,3},{3,2},{4,5},{5,4},{6,7},{7,6},{8,9},{9,8},{10,11... | collective-permute-start | bytes 3932168 | tf_op jit(solution)/shard_map/ppermute | solution.py:185
  203.8 3.4 collective-permute-start.35
  204.2 33.4 %collective-permute-start.36 = (bf16[512,1280]{1,0:T(8,128)(2,1)}, bf16[512,1280]{1,0:T(8,128)(2,1)S(1)}, u32[]{:S(2)}, u32[]{:S(2)}) collective-permute-start(bf16[512,1280]{1,0:T(8,128)(2,1)} %add_convert_fusion.1), channel_id=1, source_target_pairs={{0,2},{1,3},{2,0},{3,1},{4,6},{5,7},{6,4},{7,5},{8,10},{9,11},{10,... | collective-permute-start | bytes 3932168 | tf_op jit(solution)/shard_map/ppermute | solution.py:185
  220.3 20.8 %collective-permute-start.37 = (bf16[320,1280]{1,0:T(8,128)(2,1)}, bf16[320,1280]{1,0:T(8,128)(2,1)}, u32[]{:S(2)}, u32[]{:S(2)}) collective-permute-start(bf16[320,1280]{1,0:T(8,128)(2,1)} %pad_maximum_fusion.6), channel_id=1, source_target_pairs={{0,4},{4,0},{8,12},{12,8},{16,20},{20,16},{24,28},{28,24},{1,5},{5... | collective-permute-start | bytes 2457608 | tf_op jit(solution)/shard_map/ppermute | solution.py:185
  245.5 6.9 %collective-permute-start.38 = (bf16[512,1280]{1,0:T(8,128)(2,1)S(1)}, bf16[512,1280]{1,0:T(8,128)(2,1)}, u32[]{:S(2)}, u32[]{:S(2)}) collective-permute-start(bf16[512,1280]{1,0:T(8,128)(2,1)S(1)} %get-tuple-element.399.own_ref.refs_2_), channel_id=1, source_target_pairs={{0,1},{1,0},{2,3},{3,2},{4,5},{5,4},{6,7},{7,6},{8,9},{9,8},{10,11... | collective-permute-start | bytes 3932168 | tf_op jit(solution)/shard_map/ppermute | solution.py:185
  245.6 6.8 %collective-permute-start.39 = (bf16[512,1280]{1,0:T(8,128)(2,1)}, bf16[512,1280]{1,0:T(8,128)(2,1)}, u32[]{:S(2)}, u32[]{:S(2)}) collective-permute-start(bf16[512,1280]{1,0:T(8,128)(2,1)} %convolution_convert_fusion.4), channel_id=1, source_target_pairs={{0,1},{1,0},{2,3},{3,2},{4,5},{5,4},{6,7},{7,6},{8,9},{9,8},{10,11... | collective-permute-start | bytes 3932168 | tf_op jit(solution)/shard_map/ppermute | solution.py:185
  246.1 6.6 %collective-permute-start.40 = (bf16[512,1280]{1,0:T(8,128)(2,1)}, bf16[512,1280]{1,0:T(8,128)(2,1)}, u32[]{:S(2)}, u32[]{:S(2)}) collective-permute-start(bf16[512,1280]{1,0:T(8,128)(2,1)} %convolution_convert_fusion.3), channel_id=1, source_target_pairs={{0,1},{1,0},{2,3},{3,2},{4,5},{5,4},{6,7},{7,6},{8,9},{9,8},{10,11... | collective-permute-start | bytes 3932168 | tf_op jit(solution)/shard_map/ppermute | solution.py:185
  246.2 31.2 %collective-permute-start.41 = (bf16[512,1280]{1,0:T(8,128)(2,1)S(1)}, bf16[512,1280]{1,0:T(8,128)(2,1)}, u32[]{:S(2)}, u32[]{:S(2)}) collective-permute-start(bf16[512,1280]{1,0:T(8,128)(2,1)S(1)} %get-tuple-element.399.own_ref.refs_2_), channel_id=1, source_target_pairs={{0,2},{1,3},{2,0},{3,1},{4,6},{5,7},{6,4},{7,5},{8,10},{9,11},{10,... | collective-permute-start | bytes 3932168 | tf_op jit(solution)/shard_map/ppermute | solution.py:185
  249.8 23.2 %collective-permute-start.42 = (bf16[320,1280]{1,0:T(8,128)(2,1)}, bf16[320,1280]{1,0:T(8,128)(2,1)}, u32[]{:S(2)}, u32[]{:S(2)}) collective-permute-start(bf16[320,1280]{1,0:T(8,128)(2,1)} %pad_maximum_fusion.7), channel_id=1, source_target_pairs={{0,4},{4,0},{8,12},{12,8},{16,20},{20,16},{24,28},{28,24},{1,5},{5... | collective-permute-start | bytes 2457608 | tf_op jit(solution)/shard_map/ppermute | solution.py:185
  253.7 23.8 %collective-permute-start.43 = (bf16[320,1280]{1,0:T(8,128)(2,1)}, bf16[320,1280]{1,0:T(8,128)(2,1)}, u32[]{:S(2)}, u32[]{:S(2)}) collective-permute-start(bf16[320,1280]{1,0:T(8,128)(2,1)} %pad_maximum_fusion.8), channel_id=1, source_target_pairs={{0,8},{4,12},{8,0},{12,4},{16,24},{20,28},{24,16},{28,20},{1,9},{5... | collective-permute-start | bytes 2457608 | tf_op jit(solution)/shard_map/ppermute | solution.py:185
  277.4 8.8 %collective-permute-start.44 = (bf16[512,1280]{1,0:T(8,128)(2,1)}, bf16[512,1280]{1,0:T(8,128)(2,1)S(1)}, u32[]{:S(2)}, u32[]{:S(2)}) collective-permute-start(bf16[512,1280]{1,0:T(8,128)(2,1)} %collective-permute-done.41.refs_4_.own_ref), channel_id=1, source_target_pairs={{0,1},{1,0},{2,3},{3,2},{4,5},{5,4},{6,7},{7,6},{8,9},{9,8},{10,11... | collective-permute-start | bytes 3932168 | tf_op jit(solution)/shard_map/ppermute | solution.py:185
  277.6 21.1 %collective-permute-start.45 = (bf16[320,1280]{1,0:T(8,128)(2,1)S(1)}, bf16[320,1280]{1,0:T(8,128)(2,1)S(1)}, u32[]{:S(2)}, u32[]{:S(2)}) collective-permute-start(bf16[320,1280]{1,0:T(8,128)(2,1)S(1)} %pad_maximum_fusion.9), channel_id=1, source_target_pairs={{0,4},{4,0},{8,12},{12,8},{16,20},{20,16},{24,28},{28,24},{1,5},{5... | collective-permute-start | bytes 2457608 | tf_op jit(solution)/shard_map/ppermute | solution.py:185
  281.0 47.7 %collective-permute-start.47 = (bf16[320,1280]{1,0:T(8,128)(2,1)}, bf16[320,1280]{1,0:T(8,128)(2,1)}, u32[]{:S(2)}, u32[]{:S(2)}) collective-permute-start(bf16[320,1280]{1,0:T(8,128)(2,1)} %pad_maximum_fusion.11), channel_id=1, source_target_pairs={{0,4},{4,0},{8,12},{12,8},{16,20},{20,16},{24,28},{28,24},{1,5},{5... | collective-permute-start | bytes 2457608 | tf_op jit(solution)/shard_map/ppermute | solution.py:185
  300.6 29.0 %collective-permute-start.46 = (bf16[320,1280]{1,0:T(8,128)(2,1)}, bf16[320,1280]{1,0:T(8,128)(2,1)}, u32[]{:S(2)}, u32[]{:S(2)}) collective-permute-start(bf16[320,1280]{1,0:T(8,128)(2,1)} %pad_maximum_fusion.10), channel_id=1, source_target_pairs={{0,8},{4,12},{8,0},{12,4},{16,24},{20,28},{24,16},{28,20},{1,9},{5... | collective-permute-start | bytes 2457608 | tf_op jit(solution)/shard_map/ppermute | solution.py:185
  300.9 30.0 %collective-permute-start.50 = (bf16[512,1280]{1,0:T(8,128)(2,1)}, bf16[512,1280]{1,0:T(8,128)(2,1)}, u32[]{:S(2)}, u32[]{:S(2)}) collective-permute-start(bf16[512,1280]{1,0:T(8,128)(2,1)} %fusion.33), channel_id=1, source_target_pairs={{0,2},{1,3},{2,0},{3,1},{4,6},{5,7},{6,4},{7,5},{8,10},{9,11},{10,... | collective-permute-start | bytes 3932168 | tf_op jit(solution)/shard_map/ppermute | solution.py:185
  304.2 25.3 %collective-permute-start.48 = (bf16[160,1280]{1,0:T(8,128)(2,1)}, bf16[160,1280]{1,0:T(8,128)(2,1)}, u32[]{:S(2)}, u32[]{:S(2)}) collective-permute-start(bf16[160,1280]{1,0:T(8,128)(2,1)} %add_convert_fusion.6), channel_id=1, source_target_pairs={{0,24},{4,28},{8,16},{12,20},{16,8},{20,12},{24,0},{28,4},{1,25},{... | collective-permute-start | bytes 1228808 | tf_op jit(solution)/shard_map/ppermute | solution.py:185
  307.2 22.4 %collective-permute-start.49 = (bf16[160,1280]{1,0:T(8,128)(2,1)}, bf16[160,1280]{1,0:T(8,128)(2,1)}, u32[]{:S(2)}, u32[]{:S(2)}) collective-permute-start(bf16[160,1280]{1,0:T(8,128)(2,1)} %pad_maximum_fusion.15), channel_id=1, source_target_pairs={{0,4},{4,0},{8,12},{12,8},{16,20},{20,16},{24,28},{28,24},{1,5},{5... | collective-permute-start | bytes 1228808 | tf_op jit(solution)/shard_map/ppermute | solution.py:185
  343.3 9.8 %collective-permute-start.51 = (bf16[512,1280]{1,0:T(8,128)(2,1)S(1)}, bf16[512,1280]{1,0:T(8,128)(2,1)S(1)}, u32[]{:S(2)}, u32[]{:S(2)}) collective-permute-start(bf16[512,1280]{1,0:T(8,128)(2,1)S(1)} %convolution_convert_fusion.2), channel_id=1, source_target_pairs={{0,1},{1,0},{2,3},{3,2},{4,5},{5,4},{6,7},{7,6},{8,9},{9,8},{10,11... | collective-permute-start | bytes 3932168 | tf_op jit(solution)/shard_map/ppermute | solution.py:185
  345.0 10.8 %collective-permute-start.52 = (bf16[512,1280]{1,0:T(8,128)(2,1)S(1)}, bf16[512,1280]{1,0:T(8,128)(2,1)S(1)}, u32[]{:S(2)}, u32[]{:S(2)}) collective-permute-start(bf16[512,1280]{1,0:T(8,128)(2,1)S(1)} %convolution_convert_fusion.1), channel_id=1, source_target_pairs={{0,1},{1,0},{2,3},{3,2},{4,5},{5,4},{6,7},{7,6},{8,9},{9,8},{10,11... | collective-permute-start | bytes 3932168 | tf_op jit(solution)/shard_map/ppermute | solution.py:185
  345.6 17.7 %collective-permute-start.54 = (bf16[320,960]{1,0:T(8,128)(2,1)S(1)}, bf16[320,960]{1,0:T(8,128)(2,1)S(1)}, u32[]{:S(2)}, u32[]{:S(2)}) collective-permute-start(bf16[320,960]{1,0:T(8,128)(2,1)S(1)} %pad_maximum_fusion.13), channel_id=1, source_target_pairs={{0,4},{4,0},{8,12},{12,8},{16,20},{20,16},{24,28},{28,24},{1,5},{5... | collective-permute-start | bytes 1843208 | tf_op jit(solution)/shard_map/ppermute | solution.py:185
  346.7 24.9 %collective-permute-start.56 = (bf16[80,1280]{1,0:T(8,128)(2,1)S(1)}, bf16[80,1280]{1,0:T(8,128)(2,1)S(1)}, u32[]{:S(2)}, u32[]{:S(2)}) collective-permute-start(bf16[80,1280]{1,0:T(8,128)(2,1)S(1)} %pad_maximum_fusion.16), channel_id=1, source_target_pairs={{0,8},{4,12},{8,0},{12,4},{16,24},{20,28},{24,16},{28,20},{1,9},{5... | collective-permute-start | bytes 614408 | tf_op jit(solution)/shard_map/ppermute | solution.py:185
  350.8 20.8 %collective-permute-start.57 = (bf16[160,1280]{1,0:T(8,128)(2,1)S(1)}, bf16[160,1280]{1,0:T(8,128)(2,1)S(1)}, u32[]{:S(2)}, u32[]{:S(2)}) collective-permute-start(bf16[160,1280]{1,0:T(8,128)(2,1)S(1)} %add_convert_fusion.3), channel_id=1, source_target_pairs={{0,24},{4,28},{8,16},{12,20},{16,8},{20,12},{24,0},{28,4},{1,25},{... | collective-permute-start | bytes 1228808 | tf_op jit(solution)/shard_map/ppermute | solution.py:185
  355.8 20.6 %collective-permute-start.53 = (bf16[320,960]{1,0:T(8,128)(2,1)S(1)}, bf16[320,960]{1,0:T(8,128)(2,1)S(1)}, u32[]{:S(2)}, u32[]{:S(2)}) collective-permute-start(bf16[320,960]{1,0:T(8,128)(2,1)S(1)} %pad_maximum_fusion.12), channel_id=1, source_target_pairs={{0,4},{4,0},{8,12},{12,8},{16,20},{20,16},{24,28},{28,24},{1,5},{5... | collective-permute-start | bytes 1843208 | tf_op jit(solution)/shard_map/ppermute | solution.py:185
  363.6 15.0 %collective-permute-start.55 = (bf16[320,960]{1,0:T(8,128)(2,1)S(1)}, bf16[320,960]{1,0:T(8,128)(2,1)S(1)}, u32[]{:S(2)}, u32[]{:S(2)}) collective-permute-start(bf16[320,960]{1,0:T(8,128)(2,1)S(1)} %pad_maximum_fusion.14), channel_id=1, source_target_pairs={{0,8},{4,12},{8,0},{12,4},{16,24},{20,28},{24,16},{28,20},{1,9},{5... | collective-permute-start | bytes 1843208 | tf_op jit(solution)/shard_map/ppermute | solution.py:185
  365.4 29.0 %collective-permute-start.59 = (bf16[512,1280]{1,0:T(8,128)(2,1)}, bf16[512,1280]{1,0:T(8,128)(2,1)}, u32[]{:S(2)}, u32[]{:S(2)}) collective-permute-start(bf16[512,1280]{1,0:T(8,128)(2,1)} %add_convert_fusion), channel_id=1, source_target_pairs={{0,2},{1,3},{2,0},{3,1},{4,6},{5,7},{6,4},{7,5},{8,10},{9,11},{10,... | collective-permute-start | bytes 3932168 | tf_op jit(solution)/shard_map/ppermute | solution.py:185
  378.9 21.7 %collective-permute-start.58 = (bf16[160,960]{1,0:T(8,128)(2,1)S(1)}, bf16[160,960]{1,0:T(8,128)(2,1)S(1)}, u32[]{:S(2)}, u32[]{:S(2)}) collective-permute-start(bf16[160,960]{1,0:T(8,128)(2,1)S(1)} %get-tuple-element.409), channel_id=1, source_target_pairs={{0,24},{4,28},{8,16},{12,20},{16,8},{20,12},{24,0},{28,4},{1,25},{... | collective-permute-start | bytes 921608 | tf_op jit(solution)/shard_map/ppermute | solution.py:185
  381.2 19.4 %collective-permute-start.60 = (bf16[40,1280]{1,0:T(8,128)(2,1)S(1)}, bf16[40,1280]{1,0:T(8,128)(2,1)S(1)}, u32[]{:S(2)}, u32[]{:S(2)}) collective-permute-start(bf16[40,1280]{1,0:T(8,128)(2,1)S(1)} %add_convert_fusion.18), channel_id=1, source_target_pairs={{0,24},{4,28},{8,16},{12,20},{16,8},{20,12},{24,0},{28,4},{1,25},{... | collective-permute-start | bytes 307208 | tf_op jit(solution)/shard_map/ppermute | solution.py:185
  403.3 3.9 collective-permute-start.63
  404.4 4.9 %collective-permute-start.64 = (f32[4,1408]{1,0:T(4,128)S(1)}, f32[4,1408]{1,0:T(4,128)S(1)}, u32[]{:S(2)}, u32[]{:S(2)}) collective-permute-start(f32[4,1408]{1,0:T(4,128)S(1)} %add.435), channel_id=1, source_target_pairs={{0,6},{1,7},{2,4},{3,5},{4,2},{5,3},{6,0},{7,1},{8,14},{9,15},{10,... | collective-permute-start | bytes 67592 | tf_op jit(solution)/shard_map/ppermute | solution.py:482
  406.3 3.8 collective-permute-start.62
  410.1 4.8 %collective-permute-start.66 = (f32[4,1408]{1,0:T(4,128)S(1)}, f32[4,1408]{1,0:T(4,128)S(1)}, u32[]{:S(2)}, u32[]{:S(2)}) collective-permute-start(f32[4,1408]{1,0:T(4,128)S(1)} %add_add_fusion.1), channel_id=1, source_target_pairs={{0,16},{4,20},{8,24},{12,28},{16,0},{20,4},{24,8},{28,12},{1,17},{... | collective-permute-start | bytes 67592 | tf_op jit(solution)/shard_map/ppermute | solution.py:185
  411.3 5.7 %collective-permute-start.67 = (f32[4,1408]{1,0:T(4,128)S(1)}, f32[4,1408]{1,0:T(4,128)S(1)}, u32[]{:S(2)}, u32[]{:S(2)}) collective-permute-start(f32[4,1408]{1,0:T(4,128)S(1)} %add_add_fusion.1), channel_id=1, source_target_pairs={{0,24},{4,28},{8,16},{12,20},{16,8},{20,12},{24,0},{28,4},{1,25},{... | collective-permute-start | bytes 67592 | tf_op jit(solution)/shard_map/ppermute | solution.py:185
  412.9 4.0 collective-permute-start.65
  (104 other events, 1402.3 us)
where the time goes:
time: 434 us; the launch traced here: 428 us
  waiting for transfers between devices  116 us (27%)
  Pallas kernels  107 us (25%)
  matrix products  80 us (18%)
  starting transfers between devices  68.8 us (16%)
  other arithmetic  32.5 us (7%)
  local copies, waits for them, and re-layouts  20.5 us (5%)
    ppermute x67, waiting for transfers between devices, swap(): return lax.ppermute(value, axis, [(i, i ^ bits) for i in range(size)])  114 us
    dot_general x22, matrix products, dot(): return lax.dot_general(left, right, dims, preferred_element_type=F32)  80 us
    ppermute x67, starting transfers between devices, swap(): return lax.ppermute(value, axis, [(i, i ^ bits) for i in range(size)])  66.8 us
    pallas_call x2, Pallas kernels, attend_back(): pl.pallas_call(functools.partial(attend_back_kernel, heads, step), out_sh...  38.2 us
    pallas_call x2, Pallas kernels, attend(): pl.pallas_call(functools.partial(attend_kernel, heads, step), out_shape=(...  25.4 us
    unnamed x207, local copies, waits for them, and re-layouts  13.2 us
    pallas_call x2, Pallas kernels, weight_grad(): pl.pallas_call(functools.partial(weight_grad_kernel, len(lefts)), grid=(r...  12.2 us
    pallas_call x1, Pallas kernels, adam_all(): pl.pallas_call(functools.partial(adam_kernel, [rate for *_, rate in weigh...  9.98 us
  transfers between devices with their start and end apart: 68, of which 33 were waited for; matrix products, arithmetic and copies ran while one was open for 19% of the time, Pallas kernels for 22%

commit v1 on v0

--- a/solution.py
+++ b/solution.py
@@ -834,13 +834,14 @@
         dqkv_far, up_got, up_received, grad_up, down_parts, grad_out, out_received, last_side
     )
 
+    grad_qkv = dot(join([one_near, one_far]), join([dqkv_near, dqkv_far]), TN).astype(BF16)
+    grad_qkv, dqkv_far, dqkv_near, grad_up, up_received, grad_out, out_received = tie(
+        rows_first(grad_qkv), dqkv_far, dqkv_near, grad_up, up_received, grad_out, out_received
+    )
     up_lines.update(scatter_lines(grad_up, light, up_received[1]))
     out_lines = scatter_lines(grad_out, order, out_received)
-    dqkv_far, dqkv_near, up_lines, out_lines = tie(dqkv_far, dqkv_near, up_lines, out_lines)
     up_parts = relay_last(up_lines, up_got)
     out_got = relay_send(out_lines)
-    grad_qkv = dot(join([one_near, one_far]), join([dqkv_near, dqkv_far]), TN).astype(BF16)
-    grad_qkv, dqkv_far, dqkv_near = tie(rows_first(grad_qkv), dqkv_far, dqkv_near)
     received = [scatter_send(grad_qkv, heavy)]
     first_mates = [mates_part(v, qkv_full, NT) for v in (dqkv_far, dqkv_near)]
     far_sum = own_sum(dqkv_far, qkv_full, first_mates[0], NT).astype(BF16)

time: 434 us -> 431 us (level)
  transfers between devices with their start and end apart: 68 -> 68, of which waited for: 33 -> 33; matrix products, arithmetic and copies ran while one was open for 19% -> 19% of each run, Pallas kernels for 22% -> 23%
where the time goes in v1:
time: 431 us; the launch traced here: 425 us
  waiting for transfers between devices  114 us (26%)
  Pallas kernels  106 us (25%)
  matrix products  79.6 us (18%)
  starting transfers between devices  68.9 us (16%)
  other arithmetic  31.5 us (7%)
  local copies, waits for them, and re-layouts  20.6 us (5%)
    ppermute x67, waiting for transfers between devices, swap(): return lax.ppermute(value, axis, [(i, i ^ bits) for i in range(size)])  112 us
    dot_general x22, matrix products, dot(): return lax.dot_general(left, right, dims, preferred_element_type=F32)  79.6 us
    ppermute x67, starting transfers between devices, swap(): return lax.ppermute(value, axis, [(i, i ^ bits) for i in range(size)])  67 us
    pallas_call x2, Pallas kernels, attend_back(): pl.pallas_call(functools.partial(attend_back_kernel, heads, step), out_sh...  38.1 us
    pallas_call x2, Pallas kernels, attend(): pl.pallas_call(functools.partial(attend_kernel, heads, step), out_shape=(...  25.4 us
    unnamed x207, local copies, waits for them, and re-layouts  13.3 us
    pallas_call x2, Pallas kernels, weight_grad(): pl.pallas_call(functools.partial(weight_grad_kernel, len(lefts)), grid=(r...  12.2 us
    pallas_call x1, Pallas kernels, adam_all(): pl.pallas_call(functools.partial(adam_kernel, [rate for *_, rate in weigh...  9.98 us
  transfers between devices with their start and end apart: 68, of which 33 were waited for; matrix products, arithmetic and copies ran while one was open for 19% of the time, Pallas kernels for 23%

profile of v1, /device:TPU:0, one launch (start us, length us, event | category | flops | bytes accessed | tf_op | source)
XLA Modules:
  0.0 424.6 jit_solution(4335006156817182995)
XLA Ops:
  3.4 2.7 collective-permute-start
  6.1 2.5 collective-permute-start.1
  15.6 4.3 %collective-permute-done.10 = bf16[1,4,160]{2,1,0:T(4,128)(2,1)S(1)} collective-permute-done((bf16[1,4,160]{2,1,0:T(4,128)(2,1)S(1)}, bf16[1,4,160]{2,1,0:T(4,128)(2,1)S(1)}, u32[]{:S(2)}, u32[]{:S(2)}) %collective-permute-start.10) | collective-permute-done | bytes 1312 | tf_op jit(solution)/shard_map/ppermute | solution.py:185
  20.7 3.7 collective-permute-done.11
  24.4 3.6 collective-permute-start.12
  28.0 1.9 convert_element_type.328.refs_0_
  39.0 3.2 collective-permute-done.4.refs_4_
  42.3 10.2 %collective-permute-done.5.refs_3_ = bf16[160,1280]{1,0:T(8,128)(2,1)S(1)} collective-permute-done((bf16[160,1280]{1,0:T(8,128)(2,1)S(1)}, bf16[160,1280]{1,0:T(8,128)(2,1)S(1)}, u32[]{:S(2)}, u32[]{:S(2)}) %collective-permute-start.5) | collective-permute-done | bytes 409632 | tf_op jit(solution)/shard_map/ppermute | solution.py:185
  54.0 3.7 collective-permute-done.7.refs_1_
  64.5 1.9 norm_tokens.3.one_ref
  66.5 4.5 %norm_tokens.2.one_ref = bf16[1024,1280]{1,0:T(8,128)(2,1)S(1)} custom-call(bf16[128,1280]{1,0:T(8,128)(2,1)} %collective-permute-done.3.refs_0_, bf16[384,1280]{1,0:T(8,128)(2,1)} %collective-permute-done.7.refs_1_, bf16[128,1280]{1,0:T(8,128)(2,1)S(1)} %copy-done.66, bf16[384,1280]{1,0:T(8,128)(2,1)} %collective-permute-done.14.refs_3_, ...), custom_call_target="tpu_custom_call" | custom-call | bytes 1 | tf_op jit(solution)/shard_map/norm_tokens/pallas_call | solution.py:427
  73.2 3.1 assemble.3
  77.9 12.7 %attend.2 = (bf16[1024,960]{1,0:T(8,128)(2,1)S(1)}, bf16[1024,320]{1,0:T(8,128)(2,1)S(1)}, f32[1024,128]{1,0:T(8,128)S(1)}) custom-call(bf16[1024,1280]{1,0:T(8,128)(2,1)S(1)} %norm_tokens.2.one_ref, bf16[1280,960]{1,0:T(8,128)(2,1)} %bitcast.49, f32[8,1024]{1,0:T(8,128)S(1)} %broadcast_in_dim.27.bias_ref), custom_call_target="tpu_custom_call" | custom-call | bytes 1 | tf_op jit(solution)/shard_map/attend/pallas_call | solution.py:90
  91.7 3.0 collective-permute-done.19
  102.1 12.7 %attend.3 = (bf16[1024,960]{1,0:T(8,128)(2,1)S(1)}, bf16[1024,320]{1,0:T(8,128)(2,1)S(1)}, f32[1024,128]{1,0:T(8,128)S(1)}) custom-call(bf16[1024,1280]{1,0:T(8,128)(2,1)S(1)} %norm_tokens.3.one_ref, bf16[1280,960]{1,0:T(8,128)(2,1)} %bitcast.50, f32[8,1024]{1,0:T(8,128)S(1)} %broadcast_in_dim.28.bias_ref), custom_call_target="tpu_custom_call" | custom-call | bytes 1 | tf_op jit(solution)/shard_map/attend/pallas_call | solution.py:90
  115.6 4.5 %collective-permute-done.23 = bf16[160,1280]{1,0:T(8,128)(2,1)S(1)} collective-permute-done((bf16[160,1280]{1,0:T(8,128)(2,1)}, bf16[160,1280]{1,0:T(8,128)(2,1)S(1)}, u32[]{:S(2)}, u32[]{:S(2)}) %collective-permute-start.23) | collective-permute-done | bytes 409632 | tf_op jit(solution)/shard_map/ppermute | solution.py:185
  120.1 7.4 %collective-permute-done.24 = bf16[160,1280]{1,0:T(8,128)(2,1)S(1)} collective-permute-done((bf16[160,1280]{1,0:T(8,128)(2,1)}, bf16[160,1280]{1,0:T(8,128)(2,1)S(1)}, u32[]{:S(2)}, u32[]{:S(2)}) %collective-permute-start.24) | collective-permute-done | bytes 409632 | tf_op jit(solution)/shard_map/ppermute | solution.py:185
  127.6 2.1 convolution_convert_fusion.7
  133.0 2.9 fusion.67
  137.4 4.5 %collective-permute-done.26.refs_7_ = bf16[160,1280]{1,0:T(8,128)(2,1)S(1)} collective-permute-done((bf16[160,1280]{1,0:T(8,128)(2,1)}, bf16[160,1280]{1,0:T(8,128)(2,1)S(1)}, u32[]{:S(2)}, u32[]{:S(2)}) %collective-permute-start.26) | collective-permute-done | bytes 409632 | tf_op jit(solution)/shard_map/ppermute | solution.py:185
  145.6 2.5 pad_maximum_fusion.2
  148.2 2.3 assemble.4
  150.7 5.1 %multiply_convert_fusion.3 = (bf16[1024,1280]{1,0:T(8,128)(2,1)}, f32[1024,1280]{1,0:T(8,128)S(1)}) fusion(bf16[1024,1280]{1,0:T(8,128)(2,1)S(1)} %pad_maximum_fusion.refs_0_, bf16[1280,1280]{1,0:T(8,128)(2,1)S(1)} %bitcast.62), kind=kOutput, calls=%fused_computation.27 | convolution fusion | flops 3361996800 | bytes 13762560 | tf_op jit(solution)/shard_map/dot_general | solution.py:35
  155.8 17.7 %collective-permute-done.31.refs_3_.refs_5_.refs_7_ = bf16[3,160,1280]{2,1,0:T(8,128)(2,1)S(1)} collective-permute-done((bf16[3,160,1280]{2,1,0:T(8,128)(2,1)S(1)}, bf16[3,160,1280]{2,1,0:T(8,128)(2,1)S(1)}, u32[]{:S(2)}, u32[]{:S(2)}) %collective-permute-start.31) | collective-permute-done | bytes 1228832 | tf_op jit(solution)/shard_map/ppermute | solution.py:185
  173.9 2.3 assemble.5
  176.2 5.5 %multiply_convert_fusion.2.refs_2_ = bf16[1024,1280]{1,0:T(8,128)(2,1)S(1)} fusion(bf16[1024,1280]{1,0:T(8,128)(2,1)S(1)} %pad_maximum_fusion.1, bf16[1280,1280]{1,0:T(8,128)(2,1)S(1)} %bitcast.56, f32[1024,1280]{1,0:T(8,128)S(1)} %get-tuple-element.432), kind=kOutput, calls=%fused_computation.26 | convolution fusion | flops 3371171840 | bytes 13762560 | tf_op jit(solution)/shard_map/dot_general | solution.py:35
  181.9 5.1 %multiply_convert_fusion = (bf16[1024,1280]{1,0:T(8,128)(2,1)}, f32[1024,1280]{1,0:T(8,128)S(1)}) fusion(bf16[1024,1280]{1,0:T(8,128)(2,1)S(1)} %pad_maximum_fusion.3.refs_1_, bf16[1280,1280]{1,0:T(8,128)(2,1)S(1)} %bitcast.63), kind=kOutput, calls=%fused_computation.23 | convolution fusion | flops 3361996800 | bytes 13762560 | tf_op jit(solution)/shard_map/dot_general | solution.py:35
  187.0 5.7 %multiply_convert_fusion.1.refs_3_ = bf16[1024,1280]{1,0:T(8,128)(2,1)S(1)} fusion(bf16[1024,1280]{1,0:T(8,128)(2,1)S(1)} %pad_maximum_fusion.2, bf16[1280,1280]{1,0:T(8,128)(2,1)S(1)} %bitcast.57, f32[1024,1280]{1,0:T(8,128)S(1)} %get-tuple-element.434), kind=kOutput, calls=%fused_computation.24 | convolution fusion | flops 3371171840 | bytes 13762560 | tf_op jit(solution)/shard_map/dot_general | solution.py:35
  192.7 1.9 convolution_convert_fusion.6
  195.2 2.7 collective-permute-done.34
  197.8 2.9 add_convert_fusion.1
  200.8 3.0 convolution_convert_fusion.5
  207.1 4.6 %convert_add_fusion.1 = f32[512,1280]{1,0:T(8,128)S(1)} fusion(bf16[512,1280]{1,0:T(8,128)(2,1)} %collective-permute-done.35, bf16[1280,1280]{1,0:T(8,128)(2,1)} %bitcast.67, bf16[1024,1280]{1,0:T(8,128)(2,1)} %copy-done.30), kind=kOutput, calls=%fused_computation.61 | convolution fusion | flops 1679032320 | bytes 8519680 | tf_op jit(solution)/shard_map/dot_general | solution.py:35
  211.8 7.4 %convolution_convert_fusion = bf16[1280,1280]{1,0:T(8,128)(2,1)S(1)} fusion(bf16[1024,1280]{1,0:T(8,128)(2,1)S(1)} %copy-done.96, bf16[1024,1280]{1,0:T(8,128)(2,1)S(1)} %copy-done.98, bf16[1024,1280]{1,0:T(8,128)(2,1)S(1)} %copy-done.82, bf16[1024,1280]{1,0:T(8,128)(2,1)S(1)} %copy-done.80), kind=kOutput, calls=%fused_computation.2 | convolution fusion | flops 6733496320 | bytes 13762560 | tf_op jit(solution)/shard_map/dot_general | solution.py:35
  222.6 2.9 convolution_convert_fusion.4
  225.6 2.9 convolution_convert_fusion.3
  229.3 8.1 %weight_grad.2 = bf16[1280,1280]{1,0:T(8,128)(2,1)S(1)} custom-call(bf16[1024,1280]{1,0:T(8,128)(2,1)S(1)} %copy-done.10, bf16[1024,1280]{1,0:T(8,128)(2,1)S(1)} %pad_maximum_fusion.3.refs_1_, bf16[1024,1280]{1,0:T(8,128)(2,1)S(1)} %copy-done.31, bf16[1024,1280]{1,0:T(8,128)(2,1)S(1)} %copy-done.33), custom_call_target="tpu_custom_call" | custom-call | bytes 1 | tf_op jit(solution)/shard_map/weight_grad/pallas_call | solution.py:453
  237.5 3.5 collective-permute-done.37
  242.8 2.8 fusion.64
  254.0 19.0 %attend_back.2 = bf16[1024,960]{1,0:T(8,128)(2,1)} custom-call(bf16[1024,960]{1,0:T(8,128)(2,1)} %copy-done.35, f32[8,1024]{1,0:T(8,128)S(1)} %broadcast_in_dim.28.bias_ref, bf16[1024,320]{1,0:T(8,128)(2,1)S(1)} %copy-done.12, f32[1024,128]{1,0:T(8,128)S(1)} %copy-done.47, bf16[512,1280]{1,0:T(8,128)(2,1)S(1)} %get-tuple-element.391.own_ref.refs_2_, ...), custom_call_target="tpu_custom_call" | custom-call | bytes 1 | tf_op jit(solution)/shard_map/attend_back/pallas_call | solution.py:169
  273.0 4.4 %collective-permute-done.41.refs_4_.own_ref = bf16[512,1280]{1,0:T(8,128)(2,1)} collective-permute-done((bf16[512,1280]{1,0:T(8,128)(2,1)S(1)}, bf16[512,1280]{1,0:T(8,128)(2,1)}, u32[]{:S(2)}, u32[]{:S(2)}) %collective-permute-start.41) | collective-permute-done | bytes 1310752 | tf_op jit(solution)/shard_map/ppermute | solution.py:185
  282.0 4.2 fusion.33
  286.3 4.1 weight_grad.3
  290.4 8.3 %collective-permute-done.45 = bf16[320,1280]{1,0:T(8,128)(2,1)S(1)} collective-permute-done((bf16[320,1280]{1,0:T(8,128)(2,1)S(1)}, bf16[320,1280]{1,0:T(8,128)(2,1)S(1)}, u32[]{:S(2)}, u32[]{:S(2)}) %collective-permute-start.45) | collective-permute-done | bytes 819232 | tf_op jit(solution)/shard_map/ppermute | solution.py:185
  302.4 1.8 add_convert_fusion.6
  304.3 2.1 collective-permute-start.48
  309.6 19.1 %attend_back.3 = bf16[1024,960]{1,0:T(8,128)(2,1)} custom-call(bf16[1024,960]{1,0:T(8,128)(2,1)} %copy-done.34, f32[8,1024]{1,0:T(8,128)S(1)} %broadcast_in_dim.27.bias_ref, bf16[1024,320]{1,0:T(8,128)(2,1)S(1)} %copy-done.15, f32[1024,128]{1,0:T(8,128)S(1)} %copy-done.45, bf16[512,1280]{1,0:T(8,128)(2,1)} %collective-permute-done.41.refs_4_.own_ref, ...), custom_call_target="tpu_custom_call" | custom-call | bytes 1 | tf_op jit(solution)/shard_map/attend_back/pallas_call | solution.py:169
  331.0 7.5 %fusion.23 = bf16[1280,960]{1,0:T(8,128)(2,1)S(1)} fusion(bf16[1024,960]{1,0:T(8,128)(2,1)} %attend_back.3, bf16[1024,960]{1,0:T(8,128)(2,1)S(1)} %copy-done.83, bf16[1024,1280]{1,0:T(8,128)(2,1)S(1)} %copy-done.8, bf16[1024,1280]{1,0:T(8,128)(2,1)S(1)} %copy-done.6), kind=kOutput, calls=%fused_computation.32 | convolution fusion | flops 5052743680 | bytes 11632640 | tf_op jit(solution)/shard_map/dot_general | solution.py:35
  344.8 1.8 collective-permute-start.56
  347.6 1.9 add_convert_fusion.3
  349.5 2.2 collective-permute-start.57
  351.7 2.7 add_convert_fusion
  355.6 3.1 convolution_add_fusion.2.near_ref
  363.7 4.8 %fusion.31 = bf16[512,1280]{1,0:T(8,128)(2,1)} fusion(f32[512,1280]{1,0:T(8,128)S(1)} %copy-done.70, bf16[1280,1280]{1,0:T(8,128)(2,1)S(1)} %bitcast.61, bf16[512,1280]{1,0:T(8,128)(2,1)} %collective-permute-done.50, bf16[512,1280]{1,0:T(8,128)(2,1)} %collective-permute-done.40, bf16[1024,1280]{1,0:T(8,128)(2,1)S(1)} %copy-done.99), kind=kOutput, calls=%fused_computation.41 | convolution fusion | flops 1681653760 | bytes 11141120 | tf_op jit(solution)/shard_map/dot_general | solution.py:35
  368.5 4.7 %collective-permute-done.53 = bf16[320,960]{1,0:T(8,128)(2,1)S(1)} collective-permute-done((bf16[320,960]{1,0:T(8,128)(2,1)S(1)}, bf16[320,960]{1,0:T(8,128)(2,1)S(1)}, u32[]{:S(2)}, u32[]{:S(2)}) %collective-permute-start.53) | collective-permute-done | bytes 614432 | tf_op jit(solution)/shard_map/ppermute | solution.py:185
  373.3 3.2 collective-permute-done.55
  376.8 2.2 collective-permute-start.58
  381.6 1.8 multiply_reduce_fusion.4
  384.8 6.5 %collective-permute-done.59.far_ref = bf16[512,1280]{1,0:T(8,128)(2,1)} collective-permute-done((bf16[512,1280]{1,0:T(8,128)(2,1)}, bf16[512,1280]{1,0:T(8,128)(2,1)}, u32[]{:S(2)}, u32[]{:S(2)}) %collective-permute-start.59) | collective-permute-done | bytes 1310752 | tf_op jit(solution)/shard_map/ppermute | solution.py:185
  391.2 6.1 %first_back.1 = (bf16[512,1280]{1,0:T(8,128)(2,1)}, f32[16,1280]{1,0:T(8,128)}) custom-call(bf16[512,1280]{1,0:T(8,128)(2,1)} %tokens_ref, f32[512,1280]{1,0:T(8,128)} %convolution_add_fusion.2.near_ref, bf16[512,1280]{1,0:T(8,128)(2,1)} %collective-permute-done.59.far_ref, f32[512,1280]{1,0:T(8,128)} %get-tuple-element.392.res_ref, ...), custom_call_target="tpu_custom_call" | custom-call | bytes 1 | tf_op jit(solution)/shard_map/first_back/pallas_call | solution.py:535
  401.2 1.9 collective-permute-start.64
  403.9 2.1 collective-permute-done.64
  411.7 2.0 collective-permute-done.67
  414.4 10.0 %adam_all.1 = (f32[3,160,320]{2,1,0:T(8,128)}, f32[3,160,320]{2,1,0:T(8,128)}, f32[3,160,320]{2,1,0:T(8,128)}, f32[40,1280]{1,0:T(8,128)}, f32[40,1280]{1,0:T(8,...) custom-call(f32[4,1408]{1,0:T(4,128)} %copy-done.91, ...), custom_call_target="tpu_custom_call" | custom-call | tf_op jit(solution)/shard_map/adam_all/pallas_call | solution.py:616
  (397 shorter events, 109.2 us)
Async XLA Ops:
  0.7 10.2 %collective-permute-start.9 = (bf16[512,1280]{1,0:T(8,128)(2,1)}, bf16[512,1280]{1,0:T(8,128)(2,1)S(1)}, u32[]{:S(2)}, u32[]{:S(2)}) collective-permute-start(bf16[512,1280]{1,0:T(8,128)(2,1)} %tokens_ref), channel_id=1, source_target_pairs={{0,1},{1,0},{2,3},{3,2},{4,5},{5,4},{6,7},{7,6},{8,9},{9,8},{10,11... | collective-permute-start | bytes 3932168 | tf_op jit(solution)/shard_map/ppermute | solution.py:185
  3.4 27.8 %collective-permute-start = (bf16[160,1280]{1,0:T(8,128)(2,1)S(1)}, bf16[160,1280]{1,0:T(8,128)(2,1)S(1)}, u32[]{:S(2)}, u32[]{:S(2)}) collective-permute-start(bf16[160,1280]{1,0:T(8,128)(2,1)S(1)} %pack_first.1.refs_0_), channel_id=1, source_target_pairs={{0,8},{4,12},{8,0},{12,4},{16,24},{20,28},{24,16},{28,20},{1,9},{5... | collective-permute-start | bytes 1228808 | tf_op jit(solution)/shard_map/ppermute | solution.py:185
  6.1 25.1 %collective-permute-start.1 = (bf16[160,1280]{1,0:T(8,128)(2,1)S(1)}, bf16[160,1280]{1,0:T(8,128)(2,1)S(1)}, u32[]{:S(2)}, u32[]{:S(2)}) collective-permute-start(bf16[160,1280]{1,0:T(8,128)(2,1)S(1)} %pack_first.1.refs_0_), channel_id=1, source_target_pairs={{0,24},{4,28},{8,16},{12,20},{16,8},{20,12},{24,0},{28,4},{1,25},{... | collective-permute-start | bytes 1228808 | tf_op jit(solution)/shard_map/ppermute | solution.py:185
  8.6 22.6 %collective-permute-start.2 = (bf16[160,1280]{1,0:T(8,128)(2,1)S(1)}, bf16[160,1280]{1,0:T(8,128)(2,1)S(1)}, u32[]{:S(2)}, u32[]{:S(2)}) collective-permute-start(bf16[160,1280]{1,0:T(8,128)(2,1)S(1)} %pack_first.1.refs_0_), channel_id=1, source_target_pairs={{0,4},{4,0},{8,12},{12,8},{16,20},{20,16},{24,28},{28,24},{1,5},{5... | collective-permute-start | bytes 1228808 | tf_op jit(solution)/shard_map/ppermute | solution.py:185
  11.9 8.0 %collective-permute-start.10 = (bf16[1,4,160]{2,1,0:T(4,128)(2,1)S(1)}, bf16[1,4,160]{2,1,0:T(4,128)(2,1)S(1)}, u32[]{:S(2)}, u32[]{:S(2)}) collective-permute-start(bf16[1,4,160]{2,1,0:T(4,128)(2,1)S(1)} %bitcast.76), channel_id=1, source_target_pairs={{0,4},{4,0},{8,12},{12,8},{16,20},{20,16},{24,28},{28,24},{1,5},{5... | collective-permute-start | bytes 3848 | tf_op jit(solution)/shard_map/ppermute | solution.py:185
  14.1 17.1 %collective-permute-start.3 = (bf16[128,1280]{1,0:T(8,128)(2,1)}, bf16[128,1280]{1,0:T(8,128)(2,1)}, u32[]{:S(2)}, u32[]{:S(2)}) collective-permute-start(bf16[128,1280]{1,0:T(8,128)(2,1)} %slice.150), channel_id=1, source_target_pairs={{0,2},{1,3},{2,0},{3,1},{4,6},{5,7},{6,4},{7,5},{8,10},{9,11},{10,... | collective-permute-start | bytes 983048 | tf_op jit(solution)/shard_map/ppermute | solution.py:185
  19.9 4.5 %collective-permute-start.11 = (bf16[2,4,160]{2,1,0:T(4,128)(2,1)S(1)}, bf16[2,4,160]{2,1,0:T(4,128)(2,1)S(1)}, u32[]{:S(2)}, u32[]{:S(2)}) collective-permute-start(bf16[2,4,160]{2,1,0:T(4,128)(2,1)S(1)} %pad_maximum_fusion.20), channel_id=1, source_target_pairs={{0,8},{4,12},{8,0},{12,4},{16,24},{20,28},{24,16},{28,20},{1,9},{5... | collective-permute-start | bytes 7688 | tf_op jit(solution)/shard_map/ppermute | solution.py:185
  24.4 12.1 %collective-permute-start.12 = (bf16[4,4,160]{2,1,0:T(4,128)(2,1)S(1)}, bf16[4,4,160]{2,1,0:T(4,128)(2,1)S(1)}, u32[]{:S(2)}, u32[]{:S(2)}) collective-permute-start(bf16[4,4,160]{2,1,0:T(4,128)(2,1)S(1)} %pad_maximum_fusion.19), channel_id=1, source_target_pairs={{0,16},{4,20},{8,24},{12,28},{16,0},{20,4},{24,8},{28,12},{1,17},{... | collective-permute-start | bytes 15368 | tf_op jit(solution)/shard_map/ppermute | solution.py:185
  31.2 11.0 %collective-permute-start.4 = (bf16[160,1280]{1,0:T(8,128)(2,1)S(1)}, bf16[160,1280]{1,0:T(8,128)(2,1)S(1)}, u32[]{:S(2)}, u32[]{:S(2)}) collective-permute-start(bf16[160,1280]{1,0:T(8,128)(2,1)S(1)} %collective-permute-done.1.refs_6_), channel_id=1, source_target_pairs={{0,8},{4,12},{8,0},{12,4},{16,24},{20,28},{24,16},{28,20},{1,9},{5... | collective-permute-start | bytes 1228808 | tf_op jit(solution)/shard_map/ppermute | solution.py:185
  32.8 20.4 %collective-permute-start.6 = (bf16[160,1280]{1,0:T(8,128)(2,1)S(1)}, bf16[160,1280]{1,0:T(8,128)(2,1)S(1)}, u32[]{:S(2)}, u32[]{:S(2)}) collective-permute-start(bf16[160,1280]{1,0:T(8,128)(2,1)S(1)} %collective-permute-done.1.refs_6_), channel_id=1, source_target_pairs={{0,4},{4,0},{8,12},{12,8},{16,20},{20,16},{24,28},{28,24},{1,5},{5... | collective-permute-start | bytes 1228808 | tf_op jit(solution)/shard_map/ppermute | solution.py:185
  34.3 18.2 %collective-permute-start.5 = (bf16[160,1280]{1,0:T(8,128)(2,1)S(1)}, bf16[160,1280]{1,0:T(8,128)(2,1)S(1)}, u32[]{:S(2)}, u32[]{:S(2)}) collective-permute-start(bf16[160,1280]{1,0:T(8,128)(2,1)S(1)} %collective-permute-done.refs_2_), channel_id=1, source_target_pairs={{0,4},{4,0},{8,12},{12,8},{16,20},{20,16},{24,28},{28,24},{1,5},{5... | collective-permute-start | bytes 1228808 | tf_op jit(solution)/shard_map/ppermute | solution.py:185
  34.9 22.8 %collective-permute-start.7 = (bf16[384,1280]{1,0:T(8,128)(2,1)S(1)}, bf16[384,1280]{1,0:T(8,128)(2,1)}, u32[]{:S(2)}, u32[]{:S(2)}) collective-permute-start(bf16[384,1280]{1,0:T(8,128)(2,1)S(1)} %slice.151), channel_id=1, source_target_pairs={{0,2},{1,3},{2,0},{3,1},{4,6},{5,7},{6,4},{7,5},{8,10},{9,11},{10,... | collective-permute-start | bytes 2949128 | tf_op jit(solution)/shard_map/ppermute | solution.py:185
  57.7 8.7 %collective-permute-start.14 = (bf16[384,1280]{1,0:T(8,128)(2,1)}, bf16[384,1280]{1,0:T(8,128)(2,1)}, u32[]{:S(2)}, u32[]{:S(2)}) collective-permute-start(bf16[384,1280]{1,0:T(8,128)(2,1)} %collective-permute-done.7.refs_1_), channel_id=1, source_target_pairs={{0,1},{1,0},{2,3},{3,2},{4,5},{5,4},{6,7},{7,6},{8,9},{9,8},{10,11... | collective-permute-start | bytes 2949128 | tf_op jit(solution)/shard_map/ppermute | solution.py:185
  57.7 33.0 %collective-permute-start.18 = (bf16[512,1280]{1,0:T(8,128)(2,1)}, bf16[512,1280]{1,0:T(8,128)(2,1)}, u32[]{:S(2)}, u32[]{:S(2)}) collective-permute-start(bf16[512,1280]{1,0:T(8,128)(2,1)} %param.20), channel_id=1, source_target_pairs={{0,2},{1,3},{2,0},{3,1},{4,6},{5,7},{6,4},{7,5},{8,10},{9,11},{10,... | collective-permute-start | bytes 3932168 | tf_op jit(solution)/shard_map/ppermute | solution.py:185
  59.7 11.9 %collective-permute-start.13 = (bf16[160,1280]{1,0:T(8,128)(2,1)}, bf16[160,1280]{1,0:T(8,128)(2,1)}, u32[]{:S(2)}, u32[]{:S(2)}) collective-permute-start(bf16[160,1280]{1,0:T(8,128)(2,1)} %copy-done.54), channel_id=1, source_target_pairs={{0,4},{4,0},{8,12},{12,8},{16,20},{20,16},{24,28},{28,24},{1,5},{5... | collective-permute-start | bytes 1228808 | tf_op jit(solution)/shard_map/ppermute | solution.py:185
  61.3 29.4 %collective-permute-start.15 = (bf16[160,1280]{1,0:T(8,128)(2,1)}, bf16[160,1280]{1,0:T(8,128)(2,1)S(1)}, u32[]{:S(2)}, u32[]{:S(2)}) collective-permute-start(bf16[160,1280]{1,0:T(8,128)(2,1)} %convert_element_type.328.refs_0_), channel_id=1, source_target_pairs={{0,8},{4,12},{8,0},{12,4},{16,24},{20,28},{24,16},{28,20},{1,9},{5... | collective-permute-start | bytes 1228808 | tf_op jit(solution)/shard_map/ppermute | solution.py:185
  61.6 29.1 %collective-permute-start.16 = (bf16[160,1280]{1,0:T(8,128)(2,1)}, bf16[160,1280]{1,0:T(8,128)(2,1)}, u32[]{:S(2)}, u32[]{:S(2)}) collective-permute-start(bf16[160,1280]{1,0:T(8,128)(2,1)} %convert_element_type.328.refs_0_), channel_id=1, source_target_pairs={{0,24},{4,28},{8,16},{12,20},{16,8},{20,12},{24,0},{28,4},{1,25},{... | collective-permute-start | bytes 1228808 | tf_op jit(solution)/shard_map/ppermute | solution.py:185
  71.6 19.1 %collective-permute-start.17 = (bf16[160,1280]{1,0:T(8,128)(2,1)}, bf16[160,1280]{1,0:T(8,128)(2,1)S(1)}, u32[]{:S(2)}, u32[]{:S(2)}) collective-permute-start(bf16[160,1280]{1,0:T(8,128)(2,1)} %convert_element_type.328.refs_0_), channel_id=1, source_target_pairs={{0,4},{4,0},{8,12},{12,8},{16,20},{20,16},{24,28},{28,24},{1,5},{5... | collective-permute-start | bytes 1228808 | tf_op jit(solution)/shard_map/ppermute | solution.py:185
  96.0 31.6 %collective-permute-start.20 = (bf16[512,1280]{1,0:T(8,128)(2,1)S(1)}, bf16[512,1280]{1,0:T(8,128)(2,1)S(1)}, u32[]{:S(2)}, u32[]{:S(2)}) collective-permute-start(bf16[512,1280]{1,0:T(8,128)(2,1)S(1)} %fusion.32), channel_id=1, source_target_pairs={{0,2},{1,3},{2,0},{3,1},{4,6},{5,7},{6,4},{7,5},{8,10},{9,11},{10,... | collective-permute-start | bytes 3932168 | tf_op jit(solution)/shard_map/ppermute | solution.py:185
  97.7 29.8 %collective-permute-start.22 = (bf16[3,160,1280]{2,1,0:T(8,128)(2,1)S(1)}, bf16[3,160,1280]{2,1,0:T(8,128)(2,1)S(1)}, u32[]{:S(2)}, u32[]{:S(2)}) collective-permute-start(bf16[3,160,1280]{2,1,0:T(8,128)(2,1)S(1)} %pad_maximum_fusion.4), channel_id=1, source_target_pairs={{0,4},{4,0},{8,12},{12,8},{16,20},{20,16},{24,28},{28,24},{1,5},{5... | collective-permute-start | bytes 3686408 | tf_op jit(solution)/shard_map/ppermute | solution.py:185
  98.8 16.8 %collective-permute-start.21 = (bf16[160,1280]{1,0:T(8,128)(2,1)}, bf16[160,1280]{1,0:T(8,128)(2,1)S(1)}, u32[]{:S(2)}, u32[]{:S(2)}) collective-permute-start(bf16[160,1280]{1,0:T(8,128)(2,1)} %collective-permute-done.16.refs_4_), channel_id=1, source_target_pairs={{0,8},{4,12},{8,0},{12,4},{16,24},{20,28},{24,16},{28,20},{1,9},{5... | collective-permute-start | bytes 1228808 | tf_op jit(solution)/shard_map/ppermute | solution.py:185
  99.1 21.0 %collective-permute-start.23 = (bf16[160,1280]{1,0:T(8,128)(2,1)}, bf16[160,1280]{1,0:T(8,128)(2,1)S(1)}, u32[]{:S(2)}, u32[]{:S(2)}) collective-permute-start(bf16[160,1280]{1,0:T(8,128)(2,1)} %copy-done.18), channel_id=1, source_target_pairs={{0,8},{4,12},{8,0},{12,4},{16,24},{20,28},{24,16},{28,20},{1,9},{5... | collective-permute-start | bytes 1228808 | tf_op jit(solution)/shard_map/ppermute | solution.py:185
  100.8 26.7 %collective-permute-start.24 = (bf16[160,1280]{1,0:T(8,128)(2,1)}, bf16[160,1280]{1,0:T(8,128)(2,1)S(1)}, u32[]{:S(2)}, u32[]{:S(2)}) collective-permute-start(bf16[160,1280]{1,0:T(8,128)(2,1)} %copy-done.18), channel_id=1, source_target_pairs={{0,24},{4,28},{8,16},{12,20},{16,8},{20,12},{24,0},{28,4},{1,25},{... | collective-permute-start | bytes 1228808 | tf_op jit(solution)/shard_map/ppermute | solution.py:185
  129.6 3.4 collective-permute-start.25
  129.9 12.1 %collective-permute-start.26 = (bf16[160,1280]{1,0:T(8,128)(2,1)}, bf16[160,1280]{1,0:T(8,128)(2,1)S(1)}, u32[]{:S(2)}, u32[]{:S(2)}) collective-permute-start(bf16[160,1280]{1,0:T(8,128)(2,1)} %copy-done.62), channel_id=1, source_target_pairs={{0,4},{4,0},{8,12},{12,8},{16,20},{20,16},{24,28},{28,24},{1,5},{5... | collective-permute-start | bytes 1228808 | tf_op jit(solution)/shard_map/ppermute | solution.py:185
  130.9 11.8 %collective-permute-start.27 = (bf16[160,1280]{1,0:T(8,128)(2,1)}, bf16[160,1280]{1,0:T(8,128)(2,1)S(1)}, u32[]{:S(2)}, u32[]{:S(2)}) collective-permute-start(bf16[160,1280]{1,0:T(8,128)(2,1)} %copy-done.89), channel_id=1, source_target_pairs={{0,8},{4,12},{8,0},{12,4},{16,24},{20,28},{24,16},{28,20},{1,9},{5... | collective-permute-start | bytes 1228808 | tf_op jit(solution)/shard_map/ppermute | solution.py:185
  130.9 14.5 %collective-permute-start.29 = (bf16[512,1280]{1,0:T(8,128)(2,1)}, bf16[512,1280]{1,0:T(8,128)(2,1)S(1)}, u32[]{:S(2)}, u32[]{:S(2)}) collective-permute-start(bf16[512,1280]{1,0:T(8,128)(2,1)} %param.20), channel_id=1, source_target_pairs={{0,1},{1,0},{2,3},{3,2},{4,5},{5,4},{6,7},{7,6},{8,9},{9,8},{10,11... | collective-permute-start | bytes 3932168 | tf_op jit(solution)/shard_map/ppermute | solution.py:185
  131.1 14.5 %collective-permute-start.30 = (bf16[512,1280]{1,0:T(8,128)(2,1)}, bf16[512,1280]{1,0:T(8,128)(2,1)S(1)}, u32[]{:S(2)}, u32[]{:S(2)}) collective-permute-start(bf16[512,1280]{1,0:T(8,128)(2,1)} %collective-permute-done.18), channel_id=1, source_target_pairs={{0,1},{1,0},{2,3},{3,2},{4,5},{5,4},{6,7},{7,6},{8,9},{9,8},{10,11... | collective-permute-start | bytes 3932168 | tf_op jit(solution)/shard_map/ppermute | solution.py:185
  142.7 7.8 %collective-permute-start.28 = (bf16[512,1280]{1,0:T(8,128)(2,1)S(1)}, bf16[512,1280]{1,0:T(8,128)(2,1)S(1)}, u32[]{:S(2)}, u32[]{:S(2)}) collective-permute-start(bf16[512,1280]{1,0:T(8,128)(2,1)S(1)} %add_convert_fusion.2), channel_id=1, source_target_pairs={{0,1},{1,0},{2,3},{3,2},{4,5},{5,4},{6,7},{7,6},{8,9},{9,8},{10,11... | collective-permute-start | bytes 3932168 | tf_op jit(solution)/shard_map/ppermute | solution.py:185
  142.7 31.2 %collective-permute-start.32 = (bf16[512,1280]{1,0:T(8,128)(2,1)S(1)}, bf16[512,1280]{1,0:T(8,128)(2,1)S(1)}, u32[]{:S(2)}, u32[]{:S(2)}) collective-permute-start(bf16[512,1280]{1,0:T(8,128)(2,1)S(1)} %add_convert_fusion.2), channel_id=1, source_target_pairs={{0,2},{1,3},{2,0},{3,1},{4,6},{5,7},{6,4},{7,5},{8,10},{9,11},{10,... | collective-permute-start | bytes 3932168 | tf_op jit(solution)/shard_map/ppermute | solution.py:185
  144.3 29.2 %collective-permute-start.31 = (bf16[3,160,1280]{2,1,0:T(8,128)(2,1)S(1)}, bf16[3,160,1280]{2,1,0:T(8,128)(2,1)S(1)}, u32[]{:S(2)}, u32[]{:S(2)}) collective-permute-start(bf16[3,160,1280]{2,1,0:T(8,128)(2,1)S(1)} %pad_maximum_fusion.5.refs_2_.refs_4_.refs_6_), channel_id=1, source_target_pairs={{0,4},{4,0},{8,12},{12,8},{16,20},{20,16},{24,28},{28,24},{1,5},{5... | collective-permute-start | bytes 3686408 | tf_op jit(solution)/shard_map/ppermute | solution.py:185
  173.9 7.8 %collective-permute-start.33 = (bf16[512,1280]{1,0:T(8,128)(2,1)S(1)}, bf16[512,1280]{1,0:T(8,128)(2,1)S(1)}, u32[]{:S(2)}, u32[]{:S(2)}) collective-permute-start(bf16[512,1280]{1,0:T(8,128)(2,1)S(1)} %collective-permute-done.32), channel_id=1, source_target_pairs={{0,1},{1,0},{2,3},{3,2},{4,5},{5,4},{6,7},{7,6},{8,9},{9,8},{10,11... | collective-permute-start | bytes 3932168 | tf_op jit(solution)/shard_map/ppermute | solution.py:185
  203.8 3.4 collective-permute-start.35
  204.1 33.4 %collective-permute-start.36 = (bf16[512,1280]{1,0:T(8,128)(2,1)}, bf16[512,1280]{1,0:T(8,128)(2,1)S(1)}, u32[]{:S(2)}, u32[]{:S(2)}) collective-permute-start(bf16[512,1280]{1,0:T(8,128)(2,1)} %add_convert_fusion.1), channel_id=1, source_target_pairs={{0,2},{1,3},{2,0},{3,1},{4,6},{5,7},{6,4},{7,5},{8,10},{9,11},{10,... | collective-permute-start | bytes 3932168 | tf_op jit(solution)/shard_map/ppermute | solution.py:185
  220.2 20.8 %collective-permute-start.37 = (bf16[320,1280]{1,0:T(8,128)(2,1)}, bf16[320,1280]{1,0:T(8,128)(2,1)}, u32[]{:S(2)}, u32[]{:S(2)}) collective-permute-start(bf16[320,1280]{1,0:T(8,128)(2,1)} %pad_maximum_fusion.6), channel_id=1, source_target_pairs={{0,4},{4,0},{8,12},{12,8},{16,20},{20,16},{24,28},{28,24},{1,5},{5... | collective-permute-start | bytes 2457608 | tf_op jit(solution)/shard_map/ppermute | solution.py:185
  245.6 6.9 %collective-permute-start.38 = (bf16[512,1280]{1,0:T(8,128)(2,1)S(1)}, bf16[512,1280]{1,0:T(8,128)(2,1)}, u32[]{:S(2)}, u32[]{:S(2)}) collective-permute-start(bf16[512,1280]{1,0:T(8,128)(2,1)S(1)} %get-tuple-element.391.own_ref.refs_2_), channel_id=1, source_target_pairs={{0,1},{1,0},{2,3},{3,2},{4,5},{5,4},{6,7},{7,6},{8,9},{9,8},{10,11... | collective-permute-start | bytes 3932168 | tf_op jit(solution)/shard_map/ppermute | solution.py:185
  245.6 6.8 %collective-permute-start.39 = (bf16[512,1280]{1,0:T(8,128)(2,1)}, bf16[512,1280]{1,0:T(8,128)(2,1)}, u32[]{:S(2)}, u32[]{:S(2)}) collective-permute-start(bf16[512,1280]{1,0:T(8,128)(2,1)} %convolution_convert_fusion.4), channel_id=1, source_target_pairs={{0,1},{1,0},{2,3},{3,2},{4,5},{5,4},{6,7},{7,6},{8,9},{9,8},{10,11... | collective-permute-start | bytes 3932168 | tf_op jit(solution)/shard_map/ppermute | solution.py:185
  246.1 6.6 %collective-permute-start.40 = (bf16[512,1280]{1,0:T(8,128)(2,1)}, bf16[512,1280]{1,0:T(8,128)(2,1)}, u32[]{:S(2)}, u32[]{:S(2)}) collective-permute-start(bf16[512,1280]{1,0:T(8,128)(2,1)} %convolution_convert_fusion.3), channel_id=1, source_target_pairs={{0,1},{1,0},{2,3},{3,2},{4,5},{5,4},{6,7},{7,6},{8,9},{9,8},{10,11... | collective-permute-start | bytes 3932168 | tf_op jit(solution)/shard_map/ppermute | solution.py:185
  246.2 31.2 %collective-permute-start.41 = (bf16[512,1280]{1,0:T(8,128)(2,1)S(1)}, bf16[512,1280]{1,0:T(8,128)(2,1)}, u32[]{:S(2)}, u32[]{:S(2)}) collective-permute-start(bf16[512,1280]{1,0:T(8,128)(2,1)S(1)} %get-tuple-element.391.own_ref.refs_2_), channel_id=1, source_target_pairs={{0,2},{1,3},{2,0},{3,1},{4,6},{5,7},{6,4},{7,5},{8,10},{9,11},{10,... | collective-permute-start | bytes 3932168 | tf_op jit(solution)/shard_map/ppermute | solution.py:185
  249.9 23.2 %collective-permute-start.42 = (bf16[320,1280]{1,0:T(8,128)(2,1)}, bf16[320,1280]{1,0:T(8,128)(2,1)}, u32[]{:S(2)}, u32[]{:S(2)}) collective-permute-start(bf16[320,1280]{1,0:T(8,128)(2,1)} %pad_maximum_fusion.7), channel_id=1, source_target_pairs={{0,4},{4,0},{8,12},{12,8},{16,20},{20,16},{24,28},{28,24},{1,5},{5... | collective-permute-start | bytes 2457608 | tf_op jit(solution)/shard_map/ppermute | solution.py:185
  253.7 23.8 %collective-permute-start.43 = (bf16[320,1280]{1,0:T(8,128)(2,1)}, bf16[320,1280]{1,0:T(8,128)(2,1)}, u32[]{:S(2)}, u32[]{:S(2)}) collective-permute-start(bf16[320,1280]{1,0:T(8,128)(2,1)} %pad_maximum_fusion.8), channel_id=1, source_target_pairs={{0,8},{4,12},{8,0},{12,4},{16,24},{20,28},{24,16},{28,20},{1,9},{5... | collective-permute-start | bytes 2457608 | tf_op jit(solution)/shard_map/ppermute | solution.py:185
  277.5 8.8 %collective-permute-start.44 = (bf16[512,1280]{1,0:T(8,128)(2,1)}, bf16[512,1280]{1,0:T(8,128)(2,1)S(1)}, u32[]{:S(2)}, u32[]{:S(2)}) collective-permute-start(bf16[512,1280]{1,0:T(8,128)(2,1)} %collective-permute-done.41.refs_4_.own_ref), channel_id=1, source_target_pairs={{0,1},{1,0},{2,3},{3,2},{4,5},{5,4},{6,7},{7,6},{8,9},{9,8},{10,11... | collective-permute-start | bytes 3932168 | tf_op jit(solution)/shard_map/ppermute | solution.py:185
  277.6 21.1 %collective-permute-start.45 = (bf16[320,1280]{1,0:T(8,128)(2,1)S(1)}, bf16[320,1280]{1,0:T(8,128)(2,1)S(1)}, u32[]{:S(2)}, u32[]{:S(2)}) collective-permute-start(bf16[320,1280]{1,0:T(8,128)(2,1)S(1)} %pad_maximum_fusion.9), channel_id=1, source_target_pairs={{0,4},{4,0},{8,12},{12,8},{16,20},{20,16},{24,28},{28,24},{1,5},{5... | collective-permute-start | bytes 2457608 | tf_op jit(solution)/shard_map/ppermute | solution.py:185
  281.0 47.6 %collective-permute-start.47 = (bf16[320,1280]{1,0:T(8,128)(2,1)}, bf16[320,1280]{1,0:T(8,128)(2,1)}, u32[]{:S(2)}, u32[]{:S(2)}) collective-permute-start(bf16[320,1280]{1,0:T(8,128)(2,1)} %pad_maximum_fusion.11), channel_id=1, source_target_pairs={{0,4},{4,0},{8,12},{12,8},{16,20},{20,16},{24,28},{28,24},{1,5},{5... | collective-permute-start | bytes 2457608 | tf_op jit(solution)/shard_map/ppermute | solution.py:185
  300.6 29.0 %collective-permute-start.46 = (bf16[320,1280]{1,0:T(8,128)(2,1)}, bf16[320,1280]{1,0:T(8,128)(2,1)}, u32[]{:S(2)}, u32[]{:S(2)}) collective-permute-start(bf16[320,1280]{1,0:T(8,128)(2,1)} %pad_maximum_fusion.10), channel_id=1, source_target_pairs={{0,8},{4,12},{8,0},{12,4},{16,24},{20,28},{24,16},{28,20},{1,9},{5... | collective-permute-start | bytes 2457608 | tf_op jit(solution)/shard_map/ppermute | solution.py:185
  300.9 30.0 %collective-permute-start.50 = (bf16[512,1280]{1,0:T(8,128)(2,1)}, bf16[512,1280]{1,0:T(8,128)(2,1)}, u32[]{:S(2)}, u32[]{:S(2)}) collective-permute-start(bf16[512,1280]{1,0:T(8,128)(2,1)} %fusion.33), channel_id=1, source_target_pairs={{0,2},{1,3},{2,0},{3,1},{4,6},{5,7},{6,4},{7,5},{8,10},{9,11},{10,... | collective-permute-start | bytes 3932168 | tf_op jit(solution)/shard_map/ppermute | solution.py:185
  304.3 25.3 %collective-permute-start.48 = (bf16[160,1280]{1,0:T(8,128)(2,1)}, bf16[160,1280]{1,0:T(8,128)(2,1)}, u32[]{:S(2)}, u32[]{:S(2)}) collective-permute-start(bf16[160,1280]{1,0:T(8,128)(2,1)} %add_convert_fusion.6), channel_id=1, source_target_pairs={{0,24},{4,28},{8,16},{12,20},{16,8},{20,12},{24,0},{28,4},{1,25},{... | collective-permute-start | bytes 1228808 | tf_op jit(solution)/shard_map/ppermute | solution.py:185
  307.2 22.4 %collective-permute-start.49 = (bf16[160,1280]{1,0:T(8,128)(2,1)}, bf16[160,1280]{1,0:T(8,128)(2,1)}, u32[]{:S(2)}, u32[]{:S(2)}) collective-permute-start(bf16[160,1280]{1,0:T(8,128)(2,1)} %pad_maximum_fusion.15), channel_id=1, source_target_pairs={{0,4},{4,0},{8,12},{12,8},{16,20},{20,16},{24,28},{28,24},{1,5},{5... | collective-permute-start | bytes 1228808 | tf_op jit(solution)/shard_map/ppermute | solution.py:185
  340.1 11.6 %collective-permute-start.51 = (bf16[512,1280]{1,0:T(8,128)(2,1)S(1)}, bf16[512,1280]{1,0:T(8,128)(2,1)S(1)}, u32[]{:S(2)}, u32[]{:S(2)}) collective-permute-start(bf16[512,1280]{1,0:T(8,128)(2,1)S(1)} %convolution_convert_fusion.2), channel_id=1, source_target_pairs={{0,1},{1,0},{2,3},{3,2},{4,5},{5,4},{6,7},{7,6},{8,9},{9,8},{10,11... | collective-permute-start | bytes 3932168 | tf_op jit(solution)/shard_map/ppermute | solution.py:185
  341.8 12.5 %collective-permute-start.52 = (bf16[512,1280]{1,0:T(8,128)(2,1)S(1)}, bf16[512,1280]{1,0:T(8,128)(2,1)S(1)}, u32[]{:S(2)}, u32[]{:S(2)}) collective-permute-start(bf16[512,1280]{1,0:T(8,128)(2,1)S(1)} %convolution_convert_fusion.1), channel_id=1, source_target_pairs={{0,1},{1,0},{2,3},{3,2},{4,5},{5,4},{6,7},{7,6},{8,9},{9,8},{10,11... | collective-permute-start | bytes 3932168 | tf_op jit(solution)/shard_map/ppermute | solution.py:185
  342.5 17.7 %collective-permute-start.54 = (bf16[320,960]{1,0:T(8,128)(2,1)S(1)}, bf16[320,960]{1,0:T(8,128)(2,1)S(1)}, u32[]{:S(2)}, u32[]{:S(2)}) collective-permute-start(bf16[320,960]{1,0:T(8,128)(2,1)S(1)} %pad_maximum_fusion.13), channel_id=1, source_target_pairs={{0,4},{4,0},{8,12},{12,8},{16,20},{20,16},{24,28},{28,24},{1,5},{5... | collective-permute-start | bytes 1843208 | tf_op jit(solution)/shard_map/ppermute | solution.py:185
  344.8 23.8 %collective-permute-start.56 = (bf16[80,1280]{1,0:T(8,128)(2,1)S(1)}, bf16[80,1280]{1,0:T(8,128)(2,1)S(1)}, u32[]{:S(2)}, u32[]{:S(2)}) collective-permute-start(bf16[80,1280]{1,0:T(8,128)(2,1)S(1)} %pad_maximum_fusion.16), channel_id=1, source_target_pairs={{0,8},{4,12},{8,0},{12,4},{16,24},{20,28},{24,16},{28,20},{1,9},{5... | collective-permute-start | bytes 614408 | tf_op jit(solution)/shard_map/ppermute | solution.py:185
  349.5 19.0 %collective-permute-start.57 = (bf16[160,1280]{1,0:T(8,128)(2,1)S(1)}, bf16[160,1280]{1,0:T(8,128)(2,1)S(1)}, u32[]{:S(2)}, u32[]{:S(2)}) collective-permute-start(bf16[160,1280]{1,0:T(8,128)(2,1)S(1)} %get-tuple-element.393), channel_id=1, source_target_pairs={{0,24},{4,28},{8,16},{12,20},{16,8},{20,12},{24,0},{28,4},{1,25},{... | collective-permute-start | bytes 1228808 | tf_op jit(solution)/shard_map/ppermute | solution.py:185
  354.5 18.8 %collective-permute-start.53 = (bf16[320,960]{1,0:T(8,128)(2,1)S(1)}, bf16[320,960]{1,0:T(8,128)(2,1)S(1)}, u32[]{:S(2)}, u32[]{:S(2)}) collective-permute-start(bf16[320,960]{1,0:T(8,128)(2,1)S(1)} %pad_maximum_fusion.12), channel_id=1, source_target_pairs={{0,4},{4,0},{8,12},{12,8},{16,20},{20,16},{24,28},{28,24},{1,5},{5... | collective-permute-start | bytes 1843208 | tf_op jit(solution)/shard_map/ppermute | solution.py:185
  360.5 16.0 %collective-permute-start.55 = (bf16[320,960]{1,0:T(8,128)(2,1)S(1)}, bf16[320,960]{1,0:T(8,128)(2,1)S(1)}, u32[]{:S(2)}, u32[]{:S(2)}) collective-permute-start(bf16[320,960]{1,0:T(8,128)(2,1)S(1)} %pad_maximum_fusion.14), channel_id=1, source_target_pairs={{0,8},{4,12},{8,0},{12,4},{16,24},{20,28},{24,16},{28,20},{1,9},{5... | collective-permute-start | bytes 1843208 | tf_op jit(solution)/shard_map/ppermute | solution.py:185
  362.2 29.0 %collective-permute-start.59 = (bf16[512,1280]{1,0:T(8,128)(2,1)}, bf16[512,1280]{1,0:T(8,128)(2,1)}, u32[]{:S(2)}, u32[]{:S(2)}) collective-permute-start(bf16[512,1280]{1,0:T(8,128)(2,1)} %add_convert_fusion), channel_id=1, source_target_pairs={{0,2},{1,3},{2,0},{3,1},{4,6},{5,7},{6,4},{7,5},{8,10},{9,11},{10,... | collective-permute-start | bytes 3932168 | tf_op jit(solution)/shard_map/ppermute | solution.py:185
  376.8 20.5 %collective-permute-start.58 = (bf16[160,960]{1,0:T(8,128)(2,1)S(1)}, bf16[160,960]{1,0:T(8,128)(2,1)S(1)}, u32[]{:S(2)}, u32[]{:S(2)}) collective-permute-start(bf16[160,960]{1,0:T(8,128)(2,1)S(1)} %get-tuple-element.401), channel_id=1, source_target_pairs={{0,24},{4,28},{8,16},{12,20},{16,8},{20,12},{24,0},{28,4},{1,25},{... | collective-permute-start | bytes 921608 | tf_op jit(solution)/shard_map/ppermute | solution.py:185
  379.1 18.2 %collective-permute-start.60 = (bf16[40,1280]{1,0:T(8,128)(2,1)S(1)}, bf16[40,1280]{1,0:T(8,128)(2,1)S(1)}, u32[]{:S(2)}, u32[]{:S(2)}) collective-permute-start(bf16[40,1280]{1,0:T(8,128)(2,1)S(1)} %add_convert_fusion.18), channel_id=1, source_target_pairs={{0,24},{4,28},{8,16},{12,20},{16,8},{20,12},{24,0},{28,4},{1,25},{... | collective-permute-start | bytes 307208 | tf_op jit(solution)/shard_map/ppermute | solution.py:185
  400.1 3.9 collective-permute-start.63
  401.2 4.9 %collective-permute-start.64 = (f32[4,1408]{1,0:T(4,128)S(1)}, f32[4,1408]{1,0:T(4,128)S(1)}, u32[]{:S(2)}, u32[]{:S(2)}) collective-permute-start(f32[4,1408]{1,0:T(4,128)S(1)} %add.435), channel_id=1, source_target_pairs={{0,6},{1,7},{2,4},{3,5},{4,2},{5,3},{6,0},{7,1},{8,14},{9,15},{10,... | collective-permute-start | bytes 67592 | tf_op jit(solution)/shard_map/ppermute | solution.py:482
  403.1 3.8 collective-permute-start.62
  406.9 4.8 %collective-permute-start.66 = (f32[4,1408]{1,0:T(4,128)S(1)}, f32[4,1408]{1,0:T(4,128)S(1)}, u32[]{:S(2)}, u32[]{:S(2)}) collective-permute-start(f32[4,1408]{1,0:T(4,128)S(1)} %add_add_fusion.1), channel_id=1, source_target_pairs={{0,16},{4,20},{8,24},{12,28},{16,0},{20,4},{24,8},{28,12},{1,17},{... | collective-permute-start | bytes 67592 | tf_op jit(solution)/shard_map/ppermute | solution.py:185
  408.0 5.7 %collective-permute-start.67 = (f32[4,1408]{1,0:T(4,128)S(1)}, f32[4,1408]{1,0:T(4,128)S(1)}, u32[]{:S(2)}, u32[]{:S(2)}) collective-permute-start(f32[4,1408]{1,0:T(4,128)S(1)} %add_add_fusion.1), channel_id=1, source_target_pairs={{0,24},{4,28},{8,16},{12,20},{16,8},{20,12},{24,0},{28,4},{1,25},{... | collective-permute-start | bytes 67592 | tf_op jit(solution)/shard_map/ppermute | solution.py:185
  409.7 4.0 collective-permute-start.65
  (104 other events, 1353.5 us)
